TPU v7x, 256 devices: a whole 4x4x8 slice. The times are simulated.
256 devices in a mesh: ctx: 32 (over y, z), tp: 8 (over x, core).
Axes of the slice: x: 4, y: 4, z: 8, core: 2. Of those that a mesh axis runs over, the one named last changes fastest.
Arguments:
- inputs: bfloat16 [2, 8, 16384], P(None, None, 'ctx'), may hold values from -6 to 6
- norm_gain: float32 [16384], P('ctx'), may hold values from 0.1 to 1.9
- w_query: bfloat16 [16384, 16384], P('ctx', 'tp'), may hold values from -0.046875 to 0.046875
- w_key: bfloat16 [16384, 1024], P('ctx', 'tp'), may hold values from -0.046875 to 0.046875
- w_value: bfloat16 [16384, 1024], P('ctx', 'tp'), may hold values from -0.046875 to 0.046875
- w_out: bfloat16 [16384, 16384], P('tp', 'ctx'), may hold values from -0.046875 to 0.046875
- key_cache: bfloat16 [8, 32768, 1024], P(None, 'ctx', 'tp'), may hold values from -125 to 125
- value_cache: bfloat16 [8, 32768, 1024], P(None, 'ctx', 'tp'), may hold values from -6 to 6
Outputs:
- attended: bfloat16 [2, 8, 16384], P(None, None, 'ctx')
- new_keys: bfloat16 [2, 8, 1024], P(None, None, 'tp')
- new_values: bfloat16 [2, 8, 1024], P(None, None, 'tp')
All inputs are finite; a program needn't handle non-finite values.
Results may differ from a plain program's by a relative error of at most 0.02.
Values may be sent and summed in bfloat16 or wider, within the bound.
A program may use at most 64 MiB of HBM per device.

v0:
```python
import jax
import jax.numpy as jnp
from jax import lax
from jax.sharding import PartitionSpec as P

D = 16384
QG = 16
HD = 128
STEPS = 2


def softmax_terms(query_heads, keys_block, values_block, score_scale):
    score = (
        jnp.einsum("rgqd,rtgd->rgqt", query_heads, keys_block, preferred_element_type=jnp.float32)
        * score_scale
    )
    block_max = jnp.max(score, axis=-1)
    weight = jnp.exp(score - block_max[..., None])
    block_total = jnp.sum(weight, axis=-1)
    block_sum = jnp.einsum(
        "rgqt,rtgd->rgqd",
        weight.astype(jnp.bfloat16),
        values_block,
        preferred_element_type=jnp.float32,
    )
    return (block_max, block_total, block_sum)


def local(inputs, norm_gain, w_query, w_key, w_value, w_out, key_cache, value_cache):
    row_count = inputs.shape[1]
    kv_local = key_cache.shape[2] // HD
    cached_len = key_cache.shape[1]
    score_scale = 1.0 / float(HD) ** 0.5
    cached_keys = key_cache.reshape(row_count, cached_len, kv_local, HD)
    cached_values = value_cache.reshape(row_count, cached_len, kv_local, HD)
    attended = []
    fresh_keys = []
    fresh_values = []
    for position in range(STEPS):
        hidden = inputs[position].astype(jnp.float32)
        square_total = jnp.sum(hidden * hidden, axis=1, keepdims=True)
        normed = (hidden * norm_gain).astype(jnp.bfloat16)
        query_part = jnp.dot(normed, w_query, preferred_element_type=jnp.float32)
        key_part = jnp.dot(normed, w_key, preferred_element_type=jnp.float32)
        value_part = jnp.dot(normed, w_value, preferred_element_type=jnp.float32)
        square_total = lax.psum(square_total, "ctx")
        query_part, key_part, value_part = lax.psum((query_part, key_part, value_part), "ctx")
        scaling = lax.rsqrt(square_total / D + 1e-05)
        query = (scaling * query_part).astype(jnp.bfloat16)
        fresh_keys.append((scaling * key_part).astype(jnp.bfloat16))
        fresh_values.append((scaling * value_part).astype(jnp.bfloat16))
        query_heads = query.reshape(row_count, kv_local, QG, HD)
        stacked_keys = jnp.stack(fresh_keys, axis=1).reshape(row_count, position + 1, kv_local, HD)
        stacked_values = jnp.stack(fresh_values, axis=1).reshape(
            row_count, position + 1, kv_local, HD
        )
        local_max, local_total, local_sum = softmax_terms(
            query_heads, cached_keys, cached_values, score_scale
        )
        fresh_max, fresh_total, fresh_sum = softmax_terms(
            query_heads, stacked_keys, stacked_values, score_scale
        )
        joint_max = jnp.maximum(lax.pmax(local_max, "ctx"), fresh_max)
        local_scale = jnp.exp(local_max - joint_max)
        fresh_scale = jnp.exp(fresh_max - joint_max)
        cached_total, cached_sum = (
            lax.psum((local_total * local_scale).astype(jnp.bfloat16), "ctx").astype(jnp.float32),
            lax.psum((local_sum * local_scale[..., None]).astype(jnp.bfloat16), "ctx").astype(
                jnp.float32
            ),
        )
        joint_total = cached_total + fresh_total * fresh_scale
        joint_sum = cached_sum + fresh_sum * fresh_scale[..., None]
        heads_out = (joint_sum / joint_total[..., None]).reshape(row_count, -1).astype(jnp.bfloat16)
        partial_out = jnp.dot(heads_out, w_out, preferred_element_type=jnp.float32)
        attended.append(lax.psum(partial_out, "tp").astype(jnp.bfloat16))
    return (jnp.stack(attended), jnp.stack(fresh_keys), jnp.stack(fresh_values))


def solution(mesh):
    placed = (
        P(None, None, "ctx"),
        P("ctx"),
        P("ctx", "tp"),
        P("ctx", "tp"),
        P("ctx", "tp"),
        P("tp", "ctx"),
        P(None, "ctx", "tp"),
        P(None, "ctx", "tp"),
    )
    return jax.shard_map(
        local,
        mesh=mesh,
        in_specs=placed,
        out_specs=(P(None, None, "ctx"), P(None, None, "tp"), P(None, None, "tp")),
        check_vma=False,
    )
```

profile of v0, /device:TPU:1, one launch (start us, length us, event | category | flops | bytes accessed | tf_op | source)
XLA Modules:
  0.0 407.3 jit_solution(15208476659807938324)
XLA Ops:
  7.3 2.8 fusion.58
  10.1 1.0 fusion.64
  11.1 0.1 fusion.33
  11.3 0.1 fusion.56
  11.4 0.1 fusion.62
  11.6 0.1 fusion.54
  11.7 0.1 fusion.60
  11.8 119.0 %all-reduce = (f32[8,1]{0,1:T(1,128)S(1)}, f32[8,128]{1,0:T(8,128)S(1)}, f32[8,128]{1,0:T(8,128)S(1)}, f32[8,1]{0,1:T(1,128)S(1)}, f32[8,128]{1,0:T(8,128)S(1)}, /*index=5*/f32[8,128]{1,0:T(8,128)S(1)}) all-reduce(f32[8,1]{0,1:T(1,128)S(1)} %bitcast.184, f32[8,128]{1,0:T(8,128)S(1)} %fusion.56, ...), channel_id=1, replica_groups=mesh['ctx'=32,'tp'=8] {'ctx'}, use_global_device_ids=true, to_apply=%region_12.0 | all-reduce | flops 4112 | bytes 32896 | tf_op jit(solution)/shard_map/psum | solution.py:46
  130.8 0.1 fusion.70
  131.0 0.6 pad_maximum_fusion.3
  131.6 20.5 %all-reduce.8.cloned.1.call-done = (f32[8,2048]{1,0:T(8,128)}, f32[8,2048]{1,0:T(8,128)}) async-done(((f32[8,2048]{1,0:T(8,128)}, f32[8,2048]{1,0:T(8,128)}), (f32[8,2048]{1,0:T(8,128)}, f32[8,2048]{1,0:T(8,128)})) %all-reduce.8.cloned.1.call-update) | async-done | bytes 131088 | tf_op jit(solution)/shard_map/psum | solution.py:47
  152.1 1.0 fusion.19
  153.1 0.1 fusion.30
  153.2 0.7 fusion.76
  153.9 0.7 fusion.75
  154.7 0.2 fusion.77
  154.9 0.2 fusion.11
  155.1 0.2 fusion.9
  155.3 60.6 %all-reduce.2 = (f32[8,1,16]{2,0,1:T(8,128)S(1)}, f32[8,1,16]{2,0,1:T(8,128)S(1)}) all-reduce(f32[8,1,16]{2,0,1:T(8,128)S(1)} %bitcast.172, f32[8,1,16]{2,0,1:T(8,128)S(1)} %bitcast.171), channel_id=1, replica_groups=mesh['ctx'=32,'tp'=8] {'ctx'}, use_global_device_ids=true, to_apply=%region_15.0 | all-reduce | flops 256 | bytes 2048 | tf_op jit(solution)/shard_map/pmax | solution.py:63
  215.9 0.6 fusion.42
  216.5 2.7 fusion.7
  219.2 0.6 fusion.46
  219.8 1.1 fusion.8
  220.9 148.9 %all-reduce.10.cloned.1.call-done = (bf16[8,1,16,128]{3,2,0,1:T(8,128)(2,1)}, bf16[8,1,16]{2,0,1:T(8,128)(2,1)}, bf16[8,1,16,128]{3,2,0,1:T(8,128)(2,1)}, bf16[8,1,16]{2,0,1:T(8,128)(2,1)}) async-done(((bf16[8,1,16,128]{3,2,0,1:T(8,128)(2,1)}, bf16[8,1,16]{2,0,1:T(8,128)(2,1)}, bf16[8,1,16,128]{3,2,0,1:T(8,128)(2,1)}, bf16[8,1,16]{2,0,1:T(8,128)(2,1)}), (bf16[8,1,16,128]{3,2,0,1:T(8,128)(2,1)}, ...) | async-done | bytes 66064 | tf_op jit(solution)/shard_map/psum | solution.py:68
  369.8 0.8 fusion.45
  370.7 0.7 fusion.41
  371.3 1.0 fusion.6
  372.3 2.0 fusion.22
  374.3 0.1 fusion.21
  374.4 0.4 fusion.25
  374.8 25.1 %all-reduce.3 = (bf16[8,512]{1,0:T(8,128)(2,1)S(1)}, bf16[8,512]{1,0:T(8,128)(2,1)S(1)}) all-reduce(f32[8,512]{1,0:T(8,128)S(1)} %fusion.22, f32[8,512]{1,0:T(8,128)S(1)} %fusion.25), channel_id=1, replica_groups=mesh['ctx'=32,'tp'=8] {'tp'}, use_global_device_ids=true, to_apply=%region_23.0 | all-reduce | flops 8192 | bytes 49152 | tf_op jit(solution)/shard_map/psum | solution.py:76
  399.9 0.6 pad_maximum_fusion
  (29 shorter events, 0.3 us)
Async XLA Ops:
  7.2 146.0 %copy-start = (bf16[8,1024,128]{2,1,0:T(8,128)(2,1)S(1)}, bf16[8,1024,128]{2,1,0:T(8,128)(2,1)}, u32[]{:S(2)}) copy-start(bf16[8,1024,128]{2,1,0:T(8,128)(2,1)} %param.14) | copy-start | bytes 6291460
  7.2 2.9 copy-start.6
  7.2 2.9 copy-start.7
  7.2 144.9 %all-reduce.8.cloned.1.call-start = ((), (), s32[]{:S(2)}) async-start(), calls=%async_computation | async-start | bytes 262144 | tf_op jit(solution)/shard_map/psum | solution.py:47
  7.2 2.8 copy-start.1
  7.3 4.0 copy-start.4
  7.3 4.3 %copy-start.5 = (bf16[512,128]{1,0:T(8,128)(2,1)S(1)}, bf16[512,128]{1,0:T(8,128)(2,1)}, u32[]{:S(2)}) copy-start(bf16[512,128]{1,0:T(8,128)(2,1)} %param.12) | copy-start | bytes 393220
  11.1 358.7 %all-reduce.10.cloned.1.call-start = ((), (), s32[]{:S(2)}) async-start(), calls=%async_computation.1 | async-start | bytes 139264 | tf_op jit(solution)/shard_map/psum | solution.py:68
  215.9 3.9 copy-start.2
  369.8 4.5 %copy-start.8 = (bf16[8,1,16,128]{3,2,0,1:T(8,128)(2,1)S(1)}, bf16[8,1,16,128]{3,2,0,1:T(8,128)(2,1)}, u32[]{:S(2)}) copy-start(bf16[8,1,16,128]{3,2,0,1:T(8,128)(2,1)} %get-tuple-element.19) | copy-start | bytes 98308
  369.8 4.6 %copy-start.3 = (bf16[2048,512]{1,0:T(8,128)(2,1)S(1)}, bf16[2048,512]{1,0:T(8,128)(2,1)}, u32[]{:S(2)}) copy-start(bf16[2048,512]{1,0:T(8,128)(2,1)} %param.13) | copy-start | bytes 6291460
Sparse Core Ops, SparseCore 0:
  11.6 140.5 all-reduce.7
  221.0 148.8 all-reduce.9
where the time goes:
time: 410 us; the launch traced here: 407 us
  blocking collectives  205 us (50%)
  waiting for transfers between devices  169 us (41%)
  between operations  14.2 us (3%)
  matrix products  13.1 us (3%)
  other arithmetic  5.78 us (1%)
    psum x1, waiting for transfers between devices, local(): lax.psum((local_sum * local_scale[..., None]).astype(jnp.bfloat16), 'ctx')  149 us
    psum x1, blocking collectives, local(): square_total = lax.psum(square_total, 'ctx')  119 us
    pmax x1, blocking collectives, local(): joint_max = jnp.maximum(lax.pmax(local_max, 'ctx'), fresh_max)  60.6 us
    psum x1, blocking collectives, local(): attended.append(lax.psum(partial_out, 'tp').astype(jnp.bfloat16))  25.1 us
    psum x1, waiting for transfers between devices, local(): lax.psum((query_part, key_part, value_part), 'ctx')  20.5 us
  transfers between devices with their start and end apart: 2, of which 2 were waited for; matrix products, arithmetic and copies ran while one was open for 0% of the time, Pallas kernels for 0%

commit v1 on v0

v1 whole, which is shorter than its diff:
```python
import functools

import jax
import jax.numpy as jnp
from jax import lax
from jax.experimental import pallas as pl
from jax.experimental.pallas import tpu as pltpu
from jax.sharding import PartitionSpec as P

QG = 16
HD = 128
STEPS = 2
ROWS = 8
M = STEPS * ROWS
TILES = QG + 2
LOG2E = 1.4426950408889634
F32 = jnp.float32
BF16 = jnp.bfloat16


def owner_of(tile):
    y, j = tile // 4, lax.rem(tile, 4)
    head_owner = y * 8 + 2 * j + lax.rem(y, 2)
    return jnp.where(tile < QG, head_owner, jnp.where(tile == QG, 1, 21))


def tile_of(me):
    y, z = me // 8, lax.rem(me, 8)
    head = y * 4 + z // 2
    other = jnp.where(me == 1, QG, jnp.where(me == 21, QG + 1, TILES))
    return jnp.where(lax.rem(y + z, 2) == 0, head, other)


def kernel(
    nctx,
    ntp,
    x_hbm,
    gain_hbm,
    wq_hbm,
    wk_hbm,
    wv_hbm,
    wo_hbm,
    kc_hbm,
    vc_hbm,
    att_ref,
    nk_ref,
    nv_ref,
    x_v,
    gain_v,
    w_v,
    wo_v,
    kc_v,
    vc_v,
    sq_src,
    sq_buf,
    part_src,
    part_buf,
    proj_src,
    proj_buf,
    q_rows,
    o_rows,
    p_v,
    st_src,
    st_buf,
    o_src,
    o_buf,
    ho_src,
    ho_buf,
    fin_buf,
    load_sem,
    send_sem,
    recv_sem,
):
    me = lax.axis_index("ctx")
    tp = lax.axis_index("tp")
    depth = x_v.shape[2]
    width = wo_v.shape[1]
    mine = tile_of(me)
    owns_head = mine < QG
    owns = mine < TILES
    SQ, PART, PROJ, PROJ_KV, ST, OUT, HO, FIN = range(8)

    def load(i, src, dst):
        copy = pltpu.make_async_copy(src, dst, load_sem.at[i])
        copy.start()
        return copy

    load_x = load(0, x_hbm, x_v)
    load_gain = load(1, gain_hbm, gain_v)
    load_q = load(2, wq_hbm, w_v.at[:, pl.ds(0, QG * HD)])
    load_k = load(3, wk_hbm, w_v.at[:, pl.ds(QG * HD, HD)])
    load_v = load(4, wv_hbm, w_v.at[:, pl.ds(QG * HD + HD, HD)])
    load_kc = load(5, kc_hbm, kc_v)
    load_vc = load(6, vc_hbm, vc_v)
    load_wo = load(7, wo_hbm, wo_v)

    barrier = pltpu.get_barrier_semaphore()
    for i in range(1, nctx):
        pl.semaphore_signal(barrier, inc=1, device_id={"ctx": lax.rem(me + i, nctx)})
    for i in range(1, ntp):
        pl.semaphore_signal(barrier, inc=1, device_id={"tp": lax.rem(tp + i, ntp)})

    def send(src, dst, phase, recv, **where):
        pltpu.make_async_remote_copy(
            src_ref=src,
            dst_ref=dst,
            send_sem=send_sem.at[phase],
            recv_sem=recv_sem.at[recv],
            device_id=where,
        ).start()

    def keep(src, dst, recv):
        pltpu.make_async_copy(src, dst, recv_sem.at[recv]).start()

    def await_bytes(ref, sem):
        pltpu.make_async_copy(ref, ref, sem).wait()

    load_x.wait()
    load_gain.wait()
    x = jnp.concatenate([x_v[0].astype(F32), x_v[1].astype(F32)], axis=0)
    normed = (x * gain_v[...]).astype(BF16)
    diagonal = lax.broadcasted_iota(jnp.int32, (M, HD), 0) == lax.broadcasted_iota(
        jnp.int32, (M, HD), 1
    )
    squares = jnp.sum(x * x, axis=1, keepdims=True)
    sq_src[...] = jnp.sum(jnp.where(diagonal, squares, 0.0), axis=0, keepdims=True)
    load_q.wait()
    load_k.wait()
    load_v.wait()
    part = jnp.dot(normed, w_v[...], preferred_element_type=F32)
    for h in range(TILES):
        part_src[h] = part[:, h * HD : (h + 1) * HD]

    pl.semaphore_wait(barrier, nctx - 1 + ntp - 1)

    @pl.when(owns)
    def _():
        keep(part_src.at[mine], part_buf.at[me], PART)
        keep(sq_src, sq_buf.at[me], SQ)

    for i in range(TILES):
        h = lax.rem(me + i, TILES)
        to = owner_of(h)

        @pl.when(to != me)
        def _():
            send(part_src.at[h], part_buf.at[me], PART, PART, ctx=to)
            send(sq_src, sq_buf.at[me], SQ, SQ, ctx=to)

    @pl.when(owns)
    def _():
        await_bytes(sq_buf, recv_sem.at[SQ])
        await_bytes(part_buf, recv_sem.at[PART])
        total = jnp.sum(sq_buf[...], axis=0)
        total = jnp.sum(jnp.where(diagonal, total, 0.0), axis=1, keepdims=True)
        scaling = lax.rsqrt(total / (depth * nctx) + 1e-05)
        proj_src[...] = (scaling * jnp.sum(part_buf[...], axis=0)).astype(BF16)
        group = jnp.where(owns_head, PROJ, PROJ_KV)
        keep(proj_src, proj_buf.at[mine], group)
        for i in range(1, nctx):
            send(proj_src, proj_buf.at[mine], PROJ, group, ctx=lax.rem(me + i, nctx))

    await_bytes(proj_buf.at[pl.ds(0, QG)], recv_sem.at[PROJ])
    for h in range(QG):
        q_rows[pl.ds(h * M, M), :] = proj_buf[h].astype(F32)
    load_kc.wait()
    score_scale = LOG2E / float(HD) ** 0.5
    lane = lax.broadcasted_iota(jnp.int32, (QG, HD), 1)
    stats = jnp.zeros((QG, HD), F32)
    inverse = []
    for r in range(ROWS):
        q = jnp.concatenate(
            [q_rows[pl.ds(s * ROWS + r, QG, stride=M), :] for s in range(STEPS)], axis=0
        ).astype(BF16)
        score = lax.dot_general(
            q, kc_v[r], (((1,), (1,)), ((), ())), preferred_element_type=F32
        )
        top = jnp.max(score, axis=1, keepdims=True)
        weight = jnp.exp2((score - top) * score_scale)
        total = jnp.sum(weight, axis=1, keepdims=True)
        p_v[r] = weight.astype(BF16)
        inverse.append(1.0 / total)
        lse = top * score_scale + jnp.log2(total)
        for s in range(STEPS):
            stats = jnp.where(lane == s * ROWS + r, lse[s * QG : (s + 1) * QG], stats)
    for h in range(QG):
        st_src[h] = stats[h : h + 1]

    @pl.when(owns_head)
    def _():
        keep(st_src.at[mine], st_buf.at[me], ST)

    for i in range(QG):
        h = lax.rem(me + i, QG)
        to = owner_of(h)

        @pl.when(to != me)
        def _():
            send(st_src.at[h], st_buf.at[me], ST, ST, ctx=to)

    load_vc.wait()
    for r in range(ROWS):
        out = jnp.dot(p_v[r], vc_v[r], preferred_element_type=F32) * inverse[r]
        for s in range(STEPS):
            o_rows[pl.ds(s * ROWS + r, QG, stride=M), :] = out[s * QG : (s + 1) * QG]
    for h in range(QG):
        o_src[h] = o_rows[pl.ds(h * M, M), :].astype(BF16)

    @pl.when(owns_head)
    def _():
        keep(o_src.at[mine], o_buf.at[me], OUT)

    for i in range(QG):
        h = lax.rem(me + i, QG)
        to = owner_of(h)

        @pl.when(to != me)
        def _():
            send(o_src.at[h], o_buf.at[me], OUT, OUT, ctx=to)

    await_bytes(proj_buf.at[pl.ds(QG, 2)], recv_sem.at[PROJ_KV])
    new_k, new_v = proj_buf[QG].astype(F32), proj_buf[QG + 1].astype(F32)
    for s in range(STEPS):
        nk_ref[s] = new_k[s * ROWS : (s + 1) * ROWS].astype(BF16)
        nv_ref[s] = new_v[s * ROWS : (s + 1) * ROWS].astype(BF16)

    @pl.when(owns_head)
    def _():
        second = lax.broadcasted_iota(jnp.int32, (M, 1), 0) >= ROWS
        q = proj_src[...].astype(F32)
        k0 = jnp.concatenate([new_k[:ROWS]] * 2, axis=0)
        k1 = jnp.concatenate([new_k[ROWS:]] * 2, axis=0)
        v0 = jnp.concatenate([new_v[:ROWS]] * 2, axis=0)
        v1 = jnp.concatenate([new_v[ROWS:]] * 2, axis=0)
        f0 = jnp.sum(q * k0, axis=1, keepdims=True) * score_scale
        f1 = jnp.sum(q * k1, axis=1, keepdims=True) * score_scale
        await_bytes(st_buf, recv_sem.at[ST])
        lse = jnp.transpose(st_buf[...].reshape(nctx, HD))[:M]
        top = jnp.maximum(jnp.max(lse, axis=1, keepdims=True), f0)
        top = jnp.maximum(top, jnp.where(second, f1, f0))
        share = jnp.exp2(lse - top)
        w0 = jnp.exp2(f0 - top)
        w1 = jnp.where(second, jnp.exp2(jnp.where(second, f1, f0) - top), 0.0)
        over = 1.0 / (jnp.sum(share, axis=1, keepdims=True) + w0 + w1)
        joined = w0 * v0 + w1 * v1
        await_bytes(o_buf, recv_sem.at[OUT])
        for c in range(nctx):
            joined += share[:, c : c + 1] * o_buf[c].astype(F32)
        ho_src[...] = (joined * over).astype(BF16)
        keep(ho_src, ho_buf.at[mine], HO)
        for i in range(1, nctx):
            send(ho_src, ho_buf.at[mine], HO, HO, ctx=lax.rem(me + i, nctx))

    load_wo.wait()
    await_bytes(ho_buf, recv_sem.at[HO])
    heads_out = jnp.concatenate([ho_buf[h] for h in range(QG)], axis=1)
    y = jnp.dot(heads_out, wo_v[...], preferred_element_type=F32)
    fin_buf[tp] = y.astype(BF16)
    for i in range(1, ntp):
        send(fin_buf.at[tp], fin_buf.at[tp], FIN, FIN, tp=lax.rem(tp + i, ntp))
    await_bytes(fin_buf.at[pl.ds(0, ntp - 1)], recv_sem.at[FIN])
    att = jnp.sum(fin_buf[...].astype(F32), axis=0)
    for s in range(STEPS):
        att_ref[s] = att[s * ROWS : (s + 1) * ROWS].astype(BF16)

    @pl.when(owns)
    def _():
        await_bytes(part_src.at[pl.ds(0, TILES - 1)], send_sem.at[PART])
        await_bytes(sq_buf.at[pl.ds(0, TILES - 1)], send_sem.at[SQ])
        await_bytes(o_buf.at[pl.ds(0, nctx - 1)], send_sem.at[PROJ])

    @pl.when(jnp.logical_not(owns))
    def _():
        await_bytes(part_src, send_sem.at[PART])
        await_bytes(sq_buf.at[pl.ds(0, TILES)], send_sem.at[SQ])

    @pl.when(owns_head)
    def _():
        await_bytes(st_src.at[pl.ds(0, QG - 1)], send_sem.at[ST])
        await_bytes(o_src.at[pl.ds(0, QG - 1)], send_sem.at[OUT])
        await_bytes(o_buf.at[pl.ds(0, nctx - 1)], send_sem.at[HO])

    @pl.when(jnp.logical_not(owns_head))
    def _():
        await_bytes(st_src, send_sem.at[ST])
        await_bytes(o_src, send_sem.at[OUT])

    await_bytes(fin_buf.at[pl.ds(0, ntp - 1)], send_sem.at[FIN])


def local(nctx, ntp, inputs, norm_gain, w_query, w_key, w_value, w_out, key_cache, value_cache):
    depth = inputs.shape[2]
    width = w_out.shape[1]
    cached = key_cache.shape[1]
    hbm = pl.BlockSpec(memory_space=pl.ANY)
    vmem = pl.BlockSpec(memory_space=pltpu.VMEM)
    return pl.pallas_call(
        functools.partial(kernel, nctx, ntp),
        out_shape=(
            jax.ShapeDtypeStruct((STEPS, ROWS, width), BF16),
            jax.ShapeDtypeStruct((STEPS, ROWS, HD), BF16),
            jax.ShapeDtypeStruct((STEPS, ROWS, HD), BF16),
        ),
        in_specs=[hbm] * 8,
        out_specs=(vmem,) * 3,
        scratch_shapes=[
            pltpu.VMEM((STEPS, ROWS, depth), BF16),
            pltpu.VMEM((1, depth), F32),
            pltpu.VMEM((depth, TILES * HD), BF16),
            pltpu.VMEM((QG * HD, width), BF16),
            pltpu.VMEM((ROWS, cached, HD), BF16),
            pltpu.VMEM((ROWS, cached, HD), BF16),
            pltpu.VMEM((1, HD), F32),
            pltpu.VMEM((nctx, 1, HD), F32),
            pltpu.VMEM((TILES, M, HD), F32),
            pltpu.VMEM((nctx, M, HD), F32),
            pltpu.VMEM((M, HD), BF16),
            pltpu.VMEM((TILES, M, HD), BF16),
            pltpu.VMEM((QG * M, HD), F32),
            pltpu.VMEM((QG * M, HD), F32),
            pltpu.VMEM((ROWS, STEPS * QG, cached), BF16),
            pltpu.VMEM((QG, 1, HD), F32),
            pltpu.VMEM((nctx, 1, HD), F32),
            pltpu.VMEM((QG, M, HD), BF16),
            pltpu.VMEM((nctx, M, HD), BF16),
            pltpu.VMEM((M, HD), BF16),
            pltpu.VMEM((QG, M, HD), BF16),
            pltpu.VMEM((ntp, M, width), BF16),
            pltpu.SemaphoreType.DMA((8,)),
            pltpu.SemaphoreType.DMA((8,)),
            pltpu.SemaphoreType.DMA((8,)),
        ],
        compiler_params=pltpu.CompilerParams(
            collective_id=0, has_side_effects=True, vmem_limit_bytes=48 * 1024 * 1024
        ),
    )(
        inputs,
        norm_gain.reshape(1, depth),
        w_query,
        w_key,
        w_value,
        w_out,
        key_cache,
        value_cache,
    )


def solution(mesh):
    placed = (
        P(None, None, "ctx"),
        P("ctx"),
        P("ctx", "tp"),
        P("ctx", "tp"),
        P("ctx", "tp"),
        P("tp", "ctx"),
        P(None, "ctx", "tp"),
        P(None, "ctx", "tp"),
    )
    return jax.shard_map(
        functools.partial(local, mesh.shape["ctx"], mesh.shape["tp"]),
        mesh=mesh,
        in_specs=placed,
        out_specs=(P(None, None, "ctx"), P(None, None, "tp"), P(None, None, "tp")),
        check_vma=False,
    )
```

time: 410 us -> 54.6 us (0.13)
  blocking collectives: 205 us -> 0 us
  waiting for transfers between devices: 169 us -> 0 us
  Pallas kernels: 0 us -> 45.5 us
  between operations: 14.2 us -> 0.66 us
  matrix products: 13.1 us -> 0 us
  local copies, waits for them, and re-layouts: 0.04 us -> 8.17 us
  other arithmetic: 5.78 us -> 0 us
    psum x2 -> x0, waiting for transfers between devices: 169 us -> none  [the longest x1 149 us: local(): lax.psum((local_sum * local_scale[..., None]).astype(jnp.bfloat16), 'ctx')]
    psum x2 -> x0, blocking collectives: 144 us -> none  [the longest x1 119 us: local(): square_total = lax.psum(square_total, 'ctx')]
    pmax x1 -> x0, blocking collectives: 60.6 us -> none  [local(): joint_max = jnp.maximum(lax.pmax(local_max, 'ctx'), fresh_max)]
    pallas_call x0 -> x1, Pallas kernels: none -> 45.5 us  [local(): pl.pallas_call(functools.partial(kernel, nctx, ntp), out_shape=(jax.Shape...]
    dot_general x15 -> x0, matrix products: 13.1 us -> none  [the longest x3 4.71 us: softmax_terms(): jnp.einsum('rgqt,rtgd->rgqd', weight.astype(jnp.bfloat16), values_block,...]
    unnamed x18 -> x15, local copies, waits for them, and re-layouts: 0.04 us -> 8.17 us
  transfers between devices with their start and end apart: 2 -> 0, of which waited for: 2 -> 0; matrix products, arithmetic and copies ran while one was open for 0% -> 0% of each run, Pallas kernels for 0% -> 0%
where the time goes in v1:
time: 54.6 us; the launch traced here: 54.3 us
  Pallas kernels  45.5 us (83%)
  local copies, waits for them, and re-layouts  8.17 us (15%)
  between operations  0.66 us (1%)
    pallas_call x1, Pallas kernels, local(): pl.pallas_call(functools.partial(kernel, nctx, ntp), out_shape=(jax.Shape...  45.5 us
    unnamed x15, local copies, waits for them, and re-layouts  8.17 us

profile of v1, /device:TPU:1, one launch (start us, length us, event | category | flops | bytes accessed | tf_op | source)
XLA Modules:
  0.0 54.3 jit_solution(5311954100890653591)
XLA Ops:
  0.6 0.0 copy-start
  0.6 1.6 %copy-done = bf16[512,2048]{1,0:T(8,128)(2,1)S(1)} copy-done((bf16[512,2048]{1,0:T(8,128)(2,1)S(1)}, bf16[512,2048]{1,0:T(8,128)(2,1)}, u32[]{:S(2)}) %copy-start) | copy-done | bytes 2097176
  2.2 0.0 copy-start.1
  2.2 1.6 %copy-done.1 = bf16[2048,512]{1,0:T(8,128)(2,1)S(1)} copy-done((bf16[2048,512]{1,0:T(8,128)(2,1)S(1)}, bf16[2048,512]{1,0:T(8,128)(2,1)}, u32[]{:S(2)}) %copy-start.1) | copy-done | bytes 2097176
  3.8 0.0 copy-start.2
  3.8 0.9 %copy-done.2 = bf16[512,128]{1,0:T(8,128)(2,1)S(1)} copy-done((bf16[512,128]{1,0:T(8,128)(2,1)S(1)}, bf16[512,128]{1,0:T(8,128)(2,1)}, u32[]{:S(2)}) %copy-start.2) | copy-done | bytes 131096
  4.7 0.0 copy-start.3
  4.7 0.9 %copy-done.3 = bf16[512,128]{1,0:T(8,128)(2,1)S(1)} copy-done((bf16[512,128]{1,0:T(8,128)(2,1)S(1)}, bf16[512,128]{1,0:T(8,128)(2,1)}, u32[]{:S(2)}) %copy-start.3) | copy-done | bytes 131096
  5.6 0.0 copy-start.4
  5.6 0.7 %copy-done.4 = bf16[2,8,512]{2,1,0:T(8,128)(2,1)S(1)} copy-done((bf16[2,8,512]{2,1,0:T(8,128)(2,1)S(1)}, bf16[2,8,512]{2,1,0:T(8,128)(2,1)}, u32[]{:S(2)}) %copy-start.4) | copy-done | bytes 16408
  6.3 0.0 copy-start.5
  6.3 0.7 %copy-done.5 = f32[512]{0:T(512)S(1)} copy-done((f32[512]{0:T(512)S(1)}, f32[512]{0:T(512)}, u32[]{:S(2)}) %copy-start.5) | copy-done | bytes 2072
  7.0 45.5 %shard_map.103 = (bf16[2,8,512]{2,1,0:T(8,128)(2,1)S(1)}, bf16[2,8,128]{2,1,0:T(8,128)(2,1)S(1)}, bf16[2,8,128]{2,1,0:T(8,128)(2,1)S(1)}) custom-call(bf16[2,8,512]{2,1,0:T(8,128)(2,1)S(1)} %copy-done.4, f32[1,512]{1,0:T(1,128)S(1)} %bitcast.1, bf16[512,2048]{1,0:T(8,128)(2,1)S(1)} %copy-done, bf16[512,128]{1,0:T(8,128)(2,1)S(1)} %copy-done.2, ...), custom_call_target="tpu_custom_call" | custom-call | tf_op jit(solution)/shard_map/pallas_call | solution.py:297
  52.5 0.6 %copy.14 = bf16[2,8,512]{2,1,0:T(8,128)(2,1)} copy(bf16[2,8,512]{2,1,0:T(8,128)(2,1)S(1)} %get-tuple-element.6) | data formatting | bytes 32768
  53.2 0.6 %copy.15 = bf16[2,8,128]{2,1,0:T(8,128)(2,1)} copy(bf16[2,8,128]{2,1,0:T(8,128)(2,1)S(1)} %get-tuple-element.7) | data formatting | bytes 8192
  53.7 0.6 %copy.16 = bf16[2,8,128]{2,1,0:T(8,128)(2,1)} copy(bf16[2,8,128]{2,1,0:T(8,128)(2,1)S(1)} %get-tuple-element.8) | data formatting | bytes 8192
Async XLA Ops:
  0.6 1.6 %copy-start = (bf16[512,2048]{1,0:T(8,128)(2,1)S(1)}, bf16[512,2048]{1,0:T(8,128)(2,1)}, u32[]{:S(2)}) copy-start(bf16[512,2048]{1,0:T(8,128)(2,1)} %wq_hbm.1) | copy-start | bytes 6291460
  2.2 1.6 %copy-start.1 = (bf16[2048,512]{1,0:T(8,128)(2,1)S(1)}, bf16[2048,512]{1,0:T(8,128)(2,1)}, u32[]{:S(2)}) copy-start(bf16[2048,512]{1,0:T(8,128)(2,1)} %wo_hbm.1) | copy-start | bytes 6291460
  3.8 0.9 %copy-start.2 = (bf16[512,128]{1,0:T(8,128)(2,1)S(1)}, bf16[512,128]{1,0:T(8,128)(2,1)}, u32[]{:S(2)}) copy-start(bf16[512,128]{1,0:T(8,128)(2,1)} %wk_hbm.1) | copy-start | bytes 393220
  4.7 0.9 %copy-start.3 = (bf16[512,128]{1,0:T(8,128)(2,1)S(1)}, bf16[512,128]{1,0:T(8,128)(2,1)}, u32[]{:S(2)}) copy-start(bf16[512,128]{1,0:T(8,128)(2,1)} %wv_hbm.1) | copy-start | bytes 393220
  5.6 0.7 %copy-start.4 = (bf16[2,8,512]{2,1,0:T(8,128)(2,1)S(1)}, bf16[2,8,512]{2,1,0:T(8,128)(2,1)}, u32[]{:S(2)}) copy-start(bf16[2,8,512]{2,1,0:T(8,128)(2,1)} %x_hbm.1) | copy-start | bytes 49156
  6.3 0.7 %copy-start.5 = (f32[512]{0:T(512)S(1)}, f32[512]{0:T(512)}, u32[]{:S(2)}) copy-start(f32[512]{0:T(512)} %param.9) | copy-start | bytes 6148

commit v2 on v1

--- a/solution.py
+++ b/solution.py
@@ -18,17 +18,12 @@
 BF16 = jnp.bfloat16
 
 
-def owner_of(tile):
-    y, j = tile // 4, lax.rem(tile, 4)
-    head_owner = y * 8 + 2 * j + lax.rem(y, 2)
-    return jnp.where(tile < QG, head_owner, jnp.where(tile == QG, 1, 21))
-
-
-def tile_of(me):
-    y, z = me // 8, lax.rem(me, 8)
-    head = y * 4 + z // 2
-    other = jnp.where(me == 1, QG, jnp.where(me == 21, QG + 1, TILES))
-    return jnp.where(lax.rem(y + z, 2) == 0, head, other)
+STEPS_AWAY = sorted(
+    ((dy, dz) for dy in range(4) for dz in range(8) if (dy, dz) != (0, 0)),
+    key=lambda step: -(min(step[0], 4 - step[0]) + min(step[1], 8 - step[1])),
+)
+NEAR = 4
+KEY_OWNER, VALUE_OWNER = 0, 8
 
 
 def kernel(
@@ -47,7 +42,8 @@
     nv_ref,
     x_v,
     gain_v,
-    w_v,
+    wq_v,
+    wkv_v,
     wo_v,
     kc_v,
     vc_v,
@@ -55,7 +51,9 @@
     sq_buf,
     part_src,
     part_buf,
+    kv_buf,
     proj_src,
+    kv_src,
     proj_buf,
     q_rows,
     o_rows,
@@ -73,12 +71,11 @@
 ):
     me = lax.axis_index("ctx")
     tp = lax.axis_index("tp")
+    y, z = me // 8, lax.rem(me, 8)
     depth = x_v.shape[2]
-    width = wo_v.shape[1]
-    mine = tile_of(me)
-    owns_head = mine < QG
-    owns = mine < TILES
-    SQ, PART, PROJ, PROJ_KV, ST, OUT, HO, FIN = range(8)
+    mine = y * NEAR + z
+    owns = z < NEAR
+    SQ, PART, PART_KV, PROJ, PROJ_KV, ST, OUT, HO, FIN = range(9)
 
     def load(i, src, dst):
         copy = pltpu.make_async_copy(src, dst, load_sem.at[i])
@@ -87,18 +84,32 @@
 
     load_x = load(0, x_hbm, x_v)
     load_gain = load(1, gain_hbm, gain_v)
-    load_q = load(2, wq_hbm, w_v.at[:, pl.ds(0, QG * HD)])
-    load_k = load(3, wk_hbm, w_v.at[:, pl.ds(QG * HD, HD)])
-    load_v = load(4, wv_hbm, w_v.at[:, pl.ds(QG * HD + HD, HD)])
-    load_kc = load(5, kc_hbm, kc_v)
-    load_vc = load(6, vc_hbm, vc_v)
-    load_wo = load(7, wo_hbm, wo_v)
+    chunk = depth // 4
+    load_q = [
+        load(2 + i, wq_hbm.at[pl.ds(i * chunk, chunk)], wq_v.at[pl.ds(i * chunk, chunk)])
+        for i in range(4)
+    ]
+    load_k = load(6, wk_hbm, wkv_v.at[:, pl.ds(0, HD)])
+    load_v = load(7, wv_hbm, wkv_v.at[:, pl.ds(HD, HD)])
+
+    def others():
+        for dy, dz in STEPS_AWAY:
+            ty, tz = lax.rem(y + dy, 4), lax.rem(z + dz, 8)
+            yield ty * 8 + tz, ty * NEAR + tz, tz < NEAR
+
+    tp_others = [
+        lax.rem(tp + i, ntp) for i in sorted(range(1, ntp), key=lambda i: abs(i - ntp / 2))
+    ]
 
     barrier = pltpu.get_barrier_semaphore()
-    for i in range(1, nctx):
-        pl.semaphore_signal(barrier, inc=1, device_id={"ctx": lax.rem(me + i, nctx)})
-    for i in range(1, ntp):
-        pl.semaphore_signal(barrier, inc=1, device_id={"tp": lax.rem(tp + i, ntp)})
+
+    @pl.when(owns)
+    def _():
+        for to, _, _ in others():
+            pl.semaphore_signal(barrier, inc=1, device_id={"ctx": to})
+
+    for to in tp_others:
+        pl.semaphore_signal(barrier, inc=1, device_id={"tp": to})
 
     def send(src, dst, phase, recv, **where):
         pltpu.make_async_remote_copy(
@@ -124,41 +135,71 @@
     )
     squares = jnp.sum(x * x, axis=1, keepdims=True)
     sq_src[...] = jnp.sum(jnp.where(diagonal, squares, 0.0), axis=0, keepdims=True)
-    load_q.wait()
+    for copy in load_q:
+        copy.wait()
     load_k.wait()
     load_v.wait()
-    part = jnp.dot(normed, w_v[...], preferred_element_type=F32)
-    for h in range(TILES):
+    load_kc = load(0, kc_hbm, kc_v)
+    load_vc = load(1, vc_hbm, vc_v)
+    load_wo = load(2, wo_hbm, wo_v)
+    part = jnp.dot(normed, wq_v[...], preferred_element_type=F32)
+    for h in range(QG):
         part_src[h] = part[:, h * HD : (h + 1) * HD]
-
-    pl.semaphore_wait(barrier, nctx - 1 + ntp - 1)
-
-    @pl.when(owns)
-    def _():
-        keep(part_src.at[mine], part_buf.at[me], PART)
-        keep(sq_src, sq_buf.at[me], SQ)
-
-    for i in range(TILES):
-        h = lax.rem(me + i, TILES)
-        to = owner_of(h)
-
-        @pl.when(to != me)
+    part = jnp.dot(normed, wkv_v[...], preferred_element_type=F32)
+    for h in range(2):
+        part_src[QG + h] = part[:, h * HD : (h + 1) * HD]
+
+    @pl.when(owns)
+    def _():
+        pl.semaphore_wait(barrier, QG - 1 + ntp - 1)
+
+    @pl.when(jnp.logical_not(owns))
+    def _():
+        pl.semaphore_wait(barrier, QG + ntp - 1)
+
+    for to, h, is_owner in others():
+
+        @pl.when(is_owner)
         def _():
             send(part_src.at[h], part_buf.at[me], PART, PART, ctx=to)
             send(sq_src, sq_buf.at[me], SQ, SQ, ctx=to)
 
     @pl.when(owns)
     def _():
+        keep(part_src.at[mine], part_buf.at[me], PART)
+        keep(sq_src, sq_buf.at[me], SQ)
+
+    for tile, owner in ((QG, KEY_OWNER), (QG + 1, VALUE_OWNER)):
+
+        @pl.when(me != owner)
+        def _():
+            send(part_src.at[tile], kv_buf.at[me], PART_KV, PART_KV, ctx=owner)
+
+        @pl.when(me == owner)
+        def _():
+            keep(part_src.at[tile], kv_buf.at[me], PART_KV)
+
+    @pl.when(owns)
+    def _():
         await_bytes(sq_buf, recv_sem.at[SQ])
-        await_bytes(part_buf, recv_sem.at[PART])
         total = jnp.sum(sq_buf[...], axis=0)
         total = jnp.sum(jnp.where(diagonal, total, 0.0), axis=1, keepdims=True)
         scaling = lax.rsqrt(total / (depth * nctx) + 1e-05)
+        await_bytes(part_buf, recv_sem.at[PART])
         proj_src[...] = (scaling * jnp.sum(part_buf[...], axis=0)).astype(BF16)
-        group = jnp.where(owns_head, PROJ, PROJ_KV)
-        keep(proj_src, proj_buf.at[mine], group)
-        for i in range(1, nctx):
-            send(proj_src, proj_buf.at[mine], PROJ, group, ctx=lax.rem(me + i, nctx))
+        for to, _, _ in others():
+            send(proj_src, proj_buf.at[mine], PROJ, PROJ, ctx=to)
+        keep(proj_src, proj_buf.at[mine], PROJ)
+
+        for tile, owner in ((QG, KEY_OWNER), (QG + 1, VALUE_OWNER)):
+
+            @pl.when(me == owner)
+            def _():
+                await_bytes(kv_buf, recv_sem.at[PART_KV])
+                kv_src[...] = (scaling * jnp.sum(kv_buf[...], axis=0)).astype(BF16)
+                for to, _, _ in others():
+                    send(kv_src, proj_buf.at[tile], PROJ_KV, PROJ_KV, ctx=to)
+                keep(kv_src, proj_buf.at[tile], PROJ_KV)
 
     await_bytes(proj_buf.at[pl.ds(0, QG)], recv_sem.at[PROJ])
     for h in range(QG):
@@ -186,17 +227,15 @@
     for h in range(QG):
         st_src[h] = stats[h : h + 1]
 
-    @pl.when(owns_head)
-    def _():
-        keep(st_src.at[mine], st_buf.at[me], ST)
-
-    for i in range(QG):
-        h = lax.rem(me + i, QG)
-        to = owner_of(h)
-
-        @pl.when(to != me)
+    for to, h, is_owner in others():
+
+        @pl.when(is_owner)
         def _():
             send(st_src.at[h], st_buf.at[me], ST, ST, ctx=to)
+
+    @pl.when(owns)
+    def _():
+        keep(st_src.at[mine], st_buf.at[me], ST)
 
     load_vc.wait()
     for r in range(ROWS):
@@ -206,17 +245,15 @@
     for h in range(QG):
         o_src[h] = o_rows[pl.ds(h * M, M), :].astype(BF16)
 
-    @pl.when(owns_head)
-    def _():
-        keep(o_src.at[mine], o_buf.at[me], OUT)
-
-    for i in range(QG):
-        h = lax.rem(me + i, QG)
-        to = owner_of(h)
-
-        @pl.when(to != me)
+    for to, h, is_owner in others():
+
+        @pl.when(is_owner)
         def _():
             send(o_src.at[h], o_buf.at[me], OUT, OUT, ctx=to)
+
+    @pl.when(owns)
+    def _():
+        keep(o_src.at[mine], o_buf.at[me], OUT)
 
     await_bytes(proj_buf.at[pl.ds(QG, 2)], recv_sem.at[PROJ_KV])
     new_k, new_v = proj_buf[QG].astype(F32), proj_buf[QG + 1].astype(F32)
@@ -224,7 +261,7 @@
         nk_ref[s] = new_k[s * ROWS : (s + 1) * ROWS].astype(BF16)
         nv_ref[s] = new_v[s * ROWS : (s + 1) * ROWS].astype(BF16)
 
-    @pl.when(owns_head)
+    @pl.when(owns)
     def _():
         second = lax.broadcasted_iota(jnp.int32, (M, 1), 0) >= ROWS
         q = proj_src[...].astype(F32)
@@ -247,17 +284,17 @@
         for c in range(nctx):
             joined += share[:, c : c + 1] * o_buf[c].astype(F32)
         ho_src[...] = (joined * over).astype(BF16)
+        for to, _, _ in others():
+            send(ho_src, ho_buf.at[mine], HO, HO, ctx=to)
         keep(ho_src, ho_buf.at[mine], HO)
-        for i in range(1, nctx):
-            send(ho_src, ho_buf.at[mine], HO, HO, ctx=lax.rem(me + i, nctx))
 
     load_wo.wait()
     await_bytes(ho_buf, recv_sem.at[HO])
     heads_out = jnp.concatenate([ho_buf[h] for h in range(QG)], axis=1)
     y = jnp.dot(heads_out, wo_v[...], preferred_element_type=F32)
     fin_buf[tp] = y.astype(BF16)
-    for i in range(1, ntp):
-        send(fin_buf.at[tp], fin_buf.at[tp], FIN, FIN, tp=lax.rem(tp + i, ntp))
+    for to in tp_others:
+        send(fin_buf.at[tp], fin_buf.at[tp], FIN, FIN, tp=to)
     await_bytes(fin_buf.at[pl.ds(0, ntp - 1)], recv_sem.at[FIN])
     att = jnp.sum(fin_buf[...].astype(F32), axis=0)
     for s in range(STEPS):
@@ -265,25 +302,30 @@
 
     @pl.when(owns)
     def _():
-        await_bytes(part_src.at[pl.ds(0, TILES - 1)], send_sem.at[PART])
-        await_bytes(sq_buf.at[pl.ds(0, TILES - 1)], send_sem.at[SQ])
+        await_bytes(part_src.at[pl.ds(0, QG - 1)], send_sem.at[PART])
+        await_bytes(sq_buf.at[pl.ds(0, QG - 1)], send_sem.at[SQ])
         await_bytes(o_buf.at[pl.ds(0, nctx - 1)], send_sem.at[PROJ])
-
-    @pl.when(jnp.logical_not(owns))
-    def _():
-        await_bytes(part_src, send_sem.at[PART])
-        await_bytes(sq_buf.at[pl.ds(0, TILES)], send_sem.at[SQ])
-
-    @pl.when(owns_head)
-    def _():
         await_bytes(st_src.at[pl.ds(0, QG - 1)], send_sem.at[ST])
         await_bytes(o_src.at[pl.ds(0, QG - 1)], send_sem.at[OUT])
         await_bytes(o_buf.at[pl.ds(0, nctx - 1)], send_sem.at[HO])
 
-    @pl.when(jnp.logical_not(owns_head))
-    def _():
+    @pl.when(jnp.logical_not(owns))
+    def _():
+        await_bytes(part_src.at[pl.ds(0, QG)], send_sem.at[PART])
+        await_bytes(sq_buf.at[pl.ds(0, QG)], send_sem.at[SQ])
         await_bytes(st_src, send_sem.at[ST])
         await_bytes(o_src, send_sem.at[OUT])
+
+    owns_kv = jnp.logical_or(me == KEY_OWNER, me == VALUE_OWNER)
+
+    @pl.when(owns_kv)
+    def _():
+        await_bytes(part_src.at[pl.ds(0, 1)], send_sem.at[PART_KV])
+        await_bytes(o_buf.at[pl.ds(0, nctx - 1)], send_sem.at[PROJ_KV])
+
+    @pl.when(jnp.logical_not(owns_kv))
+    def _():
+        await_bytes(part_src.at[pl.ds(0, 2)], send_sem.at[PART_KV])
 
     await_bytes(fin_buf.at[pl.ds(0, ntp - 1)], send_sem.at[FIN])
 
@@ -292,21 +334,23 @@
     depth = inputs.shape[2]
     width = w_out.shape[1]
     cached = key_cache.shape[1]
-    hbm = pl.BlockSpec(memory_space=pl.ANY)
+    hbm = pl.BlockSpec(memory_space=pltpu.HBM)
     vmem = pl.BlockSpec(memory_space=pltpu.VMEM)
-    return pl.pallas_call(
+    shapes = (
+        jax.ShapeDtypeStruct((STEPS, ROWS, width), BF16),
+        jax.ShapeDtypeStruct((STEPS, ROWS, HD), BF16),
+        jax.ShapeDtypeStruct((STEPS, ROWS, HD), BF16),
+    )
+    results = pl.pallas_call(
         functools.partial(kernel, nctx, ntp),
-        out_shape=(
-            jax.ShapeDtypeStruct((STEPS, ROWS, width), BF16),
-            jax.ShapeDtypeStruct((STEPS, ROWS, HD), BF16),
-            jax.ShapeDtypeStruct((STEPS, ROWS, HD), BF16),
-        ),
+        out_shape=shapes,
         in_specs=[hbm] * 8,
         out_specs=(vmem,) * 3,
         scratch_shapes=[
             pltpu.VMEM((STEPS, ROWS, depth), BF16),
             pltpu.VMEM((1, depth), F32),
-            pltpu.VMEM((depth, TILES * HD), BF16),
+            pltpu.VMEM((depth, QG * HD), BF16),
+            pltpu.VMEM((depth, 2 * HD), BF16),
             pltpu.VMEM((QG * HD, width), BF16),
             pltpu.VMEM((ROWS, cached, HD), BF16),
             pltpu.VMEM((ROWS, cached, HD), BF16),
@@ -314,6 +358,8 @@
             pltpu.VMEM((nctx, 1, HD), F32),
             pltpu.VMEM((TILES, M, HD), F32),
             pltpu.VMEM((nctx, M, HD), F32),
+            pltpu.VMEM((nctx, M, HD), F32),
+            pltpu.VMEM((M, HD), BF16),
             pltpu.VMEM((M, HD), BF16),
             pltpu.VMEM((TILES, M, HD), BF16),
             pltpu.VMEM((QG * M, HD), F32),
@@ -327,22 +373,28 @@
             pltpu.VMEM((QG, M, HD), BF16),
             pltpu.VMEM((ntp, M, width), BF16),
             pltpu.SemaphoreType.DMA((8,)),
-            pltpu.SemaphoreType.DMA((8,)),
-            pltpu.SemaphoreType.DMA((8,)),
+            pltpu.SemaphoreType.DMA((9,)),
+            pltpu.SemaphoreType.DMA((9,)),
         ],
         compiler_params=pltpu.CompilerParams(
-            collective_id=0, has_side_effects=True, vmem_limit_bytes=48 * 1024 * 1024
+            collective_id=0, has_side_effects=True, vmem_limit_bytes=40 * 1024 * 1024
         ),
     )(
-        inputs,
-        norm_gain.reshape(1, depth),
-        w_query,
-        w_key,
-        w_value,
-        w_out,
-        key_cache,
-        value_cache,
+        *(
+            pltpu.with_memory_space_constraint(operand, pltpu.HBM)
+            for operand in (
+                inputs,
+                norm_gain.reshape(1, depth),
+                w_query,
+                w_key,
+                w_value,
+                w_out,
+                key_cache,
+                value_cache,
+            )
+        )
     )
+    return results
 
 
 def solution(mesh):

time: 54.6 us -> 46.3 us (0.85)
  local copies, waits for them, and re-layouts: 8.17 us -> 1.79 us
  Pallas kernels: 45.5 us -> 43.7 us
    unnamed x15 -> x3, local copies, waits for them, and re-layouts: 8.17 us -> 1.79 us
    pallas_call x1, Pallas kernels: 45.5 us -> 43.7 us  [local(): pl.pallas_call(functools.partial(kernel, nctx, ntp), out_shape=shapes, in...]
where the time goes in v2:
time: 46.3 us; the launch traced here: 46.1 us
  Pallas kernels  43.7 us (94%)
  local copies, waits for them, and re-layouts  1.79 us (4%)
  between operations  0.64 us (1%)
    pallas_call x1, Pallas kernels, local(): pl.pallas_call(functools.partial(kernel, nctx, ntp), out_shape=shapes, in...  43.7 us
    unnamed x3, local copies, waits for them, and re-layouts  1.79 us

profile of v2, /device:TPU:1, one launch (start us, length us, event | category | flops | bytes accessed | tf_op | source)
XLA Modules:
  0.0 46.1 jit_solution(9054793560547128054)
XLA Ops:
  0.6 43.7 %shard_map.103 = (bf16[2,8,512]{2,1,0:T(8,128)(2,1)S(1)}, bf16[2,8,128]{2,1,0:T(8,128)(2,1)S(1)}, bf16[2,8,128]{2,1,0:T(8,128)(2,1)S(1)}) custom-call(bf16[2,8,512]{2,1,0:T(8,128)(2,1)} %x_hbm.1, f32[1,512]{1,0:T(1,128)} %bitcast.1, bf16[512,2048]{1,0:T(8,128)(2,1)} %wq_hbm.1, bf16[512,128]{1,0:T(8,128)(2,1)} %wk_hbm.1, bf16[512,128]{1,0:T(8,128)(2,1)} %wv_hbm.1, ...), custom_call_target="tpu_custom_call" | custom-call | tf_op jit(solution)/shard_map/pallas_call | solution.py:344
  44.3 0.6 %copy.14 = bf16[2,8,512]{2,1,0:T(8,128)(2,1)} copy(bf16[2,8,512]{2,1,0:T(8,128)(2,1)S(1)} %get-tuple-element.6) | data formatting | bytes 32768
  44.9 0.6 %copy.15 = bf16[2,8,128]{2,1,0:T(8,128)(2,1)} copy(bf16[2,8,128]{2,1,0:T(8,128)(2,1)S(1)} %get-tuple-element.7) | data formatting | bytes 8192
  45.5 0.6 %copy.16 = bf16[2,8,128]{2,1,0:T(8,128)(2,1)} copy(bf16[2,8,128]{2,1,0:T(8,128)(2,1)S(1)} %get-tuple-element.8) | data formatting | bytes 8192

commit v3 on v2

--- a/solution.py
+++ b/solution.py
@@ -22,10 +22,6 @@
     ((dy, dz) for dy in range(4) for dz in range(8) if (dy, dz) != (0, 0)),
     key=lambda step: -(min(step[0], 4 - step[0]) + min(step[1], 8 - step[1])),
 )
-NEAR = 4
-KEY_OWNER, VALUE_OWNER = 0, 8
-
-
 def kernel(
     nctx,
     ntp,
@@ -37,9 +33,7 @@
     wo_hbm,
     kc_hbm,
     vc_hbm,
-    att_ref,
-    nk_ref,
-    nv_ref,
+    out_ref,
     x_v,
     gain_v,
     wq_v,
@@ -71,11 +65,45 @@
 ):
     me = lax.axis_index("ctx")
     tp = lax.axis_index("tp")
-    y, z = me // 8, lax.rem(me, 8)
+    y, z, core = me // 8, lax.rem(me, 8), lax.rem(tp, 2)
+    chip_tp = tp - core
     depth = x_v.shape[2]
-    mine = y * NEAR + z
-    owns = z < NEAR
+    width = wo_v.shape[1]
     SQ, PART, PART_KV, PROJ, PROJ_KV, ST, OUT, HO, FIN = range(9)
+
+    parity = lax.rem(y + z, 2)
+    tile = y * 4 + z // 2
+    sums = core == 1
+    sums_kv = jnp.logical_and(sums, jnp.logical_and(y < 2, z < 2))
+    own_sum = jnp.logical_and(sums, parity == 1)
+    sibling_sum = jnp.logical_and(core == 0, parity == 0)
+    group_tp = chip_tp + parity
+    near = lax.rem(z + 1, 8)
+    head = y * 4 + near
+    joins = near < 4
+
+    def others():
+        for dy, dz in STEPS_AWAY:
+            ty, tz = lax.rem(y + dy, 4), lax.rem(z + dz, 8)
+            yield ty * 8 + tz, ty, tz
+
+    tp_others = [
+        lax.rem(tp + i, ntp) for i in sorted(range(1, ntp), key=lambda i: abs(i - ntp / 2))
+    ]
+
+    barrier = pltpu.get_barrier_semaphore()
+
+    @pl.when(sums)
+    def _():
+        for to, _, _ in others():
+            pl.semaphore_signal(barrier, inc=1, device_id={"ctx": to, "tp": group_tp})
+
+        @pl.when(parity == 0)
+        def _():
+            pl.semaphore_signal(barrier, inc=1, device_id={"ctx": me, "tp": group_tp})
+
+    for to in tp_others:
+        pl.semaphore_signal(barrier, inc=1, device_id={"tp": to})
 
     def load(i, src, dst):
         copy = pltpu.make_async_copy(src, dst, load_sem.at[i])
@@ -91,25 +119,6 @@
     ]
     load_k = load(6, wk_hbm, wkv_v.at[:, pl.ds(0, HD)])
     load_v = load(7, wv_hbm, wkv_v.at[:, pl.ds(HD, HD)])
-
-    def others():
-        for dy, dz in STEPS_AWAY:
-            ty, tz = lax.rem(y + dy, 4), lax.rem(z + dz, 8)
-            yield ty * 8 + tz, ty * NEAR + tz, tz < NEAR
-
-    tp_others = [
-        lax.rem(tp + i, ntp) for i in sorted(range(1, ntp), key=lambda i: abs(i - ntp / 2))
-    ]
-
-    barrier = pltpu.get_barrier_semaphore()
-
-    @pl.when(owns)
-    def _():
-        for to, _, _ in others():
-            pl.semaphore_signal(barrier, inc=1, device_id={"ctx": to})
-
-    for to in tp_others:
-        pl.semaphore_signal(barrier, inc=1, device_id={"tp": to})
 
     def send(src, dst, phase, recv, **where):
         pltpu.make_async_remote_copy(
@@ -149,37 +158,58 @@
     for h in range(2):
         part_src[QG + h] = part[:, h * HD : (h + 1) * HD]
 
-    @pl.when(owns)
+    @pl.when(own_sum)
     def _():
         pl.semaphore_wait(barrier, QG - 1 + ntp - 1)
 
-    @pl.when(jnp.logical_not(owns))
+    @pl.when(jnp.logical_not(own_sum))
     def _():
         pl.semaphore_wait(barrier, QG + ntp - 1)
 
-    for to, h, is_owner in others():
-
-        @pl.when(is_owner)
-        def _():
-            send(part_src.at[h], part_buf.at[me], PART, PART, ctx=to)
-            send(sq_src, sq_buf.at[me], SQ, SQ, ctx=to)
-
-    @pl.when(owns)
-    def _():
-        keep(part_src.at[mine], part_buf.at[me], PART)
+    for to, ty, tz in others():
+
+        @pl.when(lax.rem(ty + tz, 2) == core)
+        def _():
+            h = ty * 4 + tz // 2
+            send(part_src.at[h], part_buf.at[me], PART, PART, ctx=to, tp=chip_tp + 1)
+            send(sq_src, sq_buf.at[me], SQ, SQ, ctx=to, tp=chip_tp + 1)
+
+    @pl.when(sibling_sum)
+    def _():
+        send(part_src.at[tile], part_buf.at[me], PART, PART, tp=chip_tp + 1)
+        send(sq_src, sq_buf.at[me], SQ, SQ, tp=chip_tp + 1)
+
+    @pl.when(own_sum)
+    def _():
+        keep(part_src.at[tile], part_buf.at[me], PART)
         keep(sq_src, sq_buf.at[me], SQ)
 
-    for tile, owner in ((QG, KEY_OWNER), (QG + 1, VALUE_OWNER)):
-
-        @pl.when(me != owner)
-        def _():
-            send(part_src.at[tile], kv_buf.at[me], PART_KV, PART_KV, ctx=owner)
-
-        @pl.when(me == owner)
-        def _():
-            keep(part_src.at[tile], kv_buf.at[me], PART_KV)
-
-    @pl.when(owns)
+    own_kv = jnp.logical_and(sums_kv, own_sum)
+    for i in range(2):
+        to = 8 * i + lax.rem(i + core, 2)
+        stays = jnp.logical_and(own_kv, y == i)
+
+        @pl.when(stays)
+        def _():
+            keep(part_src.at[QG + i], kv_buf.at[me], PART_KV)
+
+        @pl.when(jnp.logical_not(stays))
+        def _():
+            send(part_src.at[QG + i], kv_buf.at[me], PART_KV, PART_KV, ctx=to, tp=chip_tp + 1)
+
+    def broadcast(src, dst, phase):
+        for to, _, _ in others():
+            send(src, dst, phase, phase, ctx=to, tp=group_tp)
+
+        @pl.when(parity == 0)
+        def _():
+            send(src, dst, phase, phase, tp=group_tp)
+
+        @pl.when(parity == 1)
+        def _():
+            keep(src, dst, phase)
+
+    @pl.when(sums)
     def _():
         await_bytes(sq_buf, recv_sem.at[SQ])
         total = jnp.sum(sq_buf[...], axis=0)
@@ -187,19 +217,13 @@
         scaling = lax.rsqrt(total / (depth * nctx) + 1e-05)
         await_bytes(part_buf, recv_sem.at[PART])
         proj_src[...] = (scaling * jnp.sum(part_buf[...], axis=0)).astype(BF16)
-        for to, _, _ in others():
-            send(proj_src, proj_buf.at[mine], PROJ, PROJ, ctx=to)
-        keep(proj_src, proj_buf.at[mine], PROJ)
-
-        for tile, owner in ((QG, KEY_OWNER), (QG + 1, VALUE_OWNER)):
-
-            @pl.when(me == owner)
-            def _():
-                await_bytes(kv_buf, recv_sem.at[PART_KV])
-                kv_src[...] = (scaling * jnp.sum(kv_buf[...], axis=0)).astype(BF16)
-                for to, _, _ in others():
-                    send(kv_src, proj_buf.at[tile], PROJ_KV, PROJ_KV, ctx=to)
-                keep(kv_src, proj_buf.at[tile], PROJ_KV)
+        broadcast(proj_src, proj_buf.at[tile], PROJ)
+
+        @pl.when(sums_kv)
+        def _():
+            await_bytes(kv_buf, recv_sem.at[PART_KV])
+            kv_src[...] = (scaling * jnp.sum(kv_buf[...], axis=0)).astype(BF16)
+            broadcast(kv_src, proj_buf.at[QG + y], PROJ_KV)
 
     await_bytes(proj_buf.at[pl.ds(0, QG)], recv_sem.at[PROJ])
     for h in range(QG):
@@ -227,15 +251,16 @@
     for h in range(QG):
         st_src[h] = stats[h : h + 1]
 
-    for to, h, is_owner in others():
-
-        @pl.when(is_owner)
-        def _():
-            send(st_src.at[h], st_buf.at[me], ST, ST, ctx=to)
-
-    @pl.when(owns)
-    def _():
-        keep(st_src.at[mine], st_buf.at[me], ST)
+    for to, ty, tz in others():
+        to_near = lax.rem(tz + 1, 8)
+
+        @pl.when(to_near < 4)
+        def _():
+            send(st_src.at[ty * 4 + to_near], st_buf.at[me], ST, ST, ctx=to)
+
+    @pl.when(joins)
+    def _():
+        keep(st_src.at[head], st_buf.at[me], ST)
 
     load_vc.wait()
     for r in range(ROWS):
@@ -245,26 +270,27 @@
     for h in range(QG):
         o_src[h] = o_rows[pl.ds(h * M, M), :].astype(BF16)
 
-    for to, h, is_owner in others():
-
-        @pl.when(is_owner)
-        def _():
-            send(o_src.at[h], o_buf.at[me], OUT, OUT, ctx=to)
-
-    @pl.when(owns)
-    def _():
-        keep(o_src.at[mine], o_buf.at[me], OUT)
+    for to, ty, tz in others():
+        to_near = lax.rem(tz + 1, 8)
+
+        @pl.when(to_near < 4)
+        def _():
+            send(o_src.at[ty * 4 + to_near], o_buf.at[me], OUT, OUT, ctx=to)
+
+    @pl.when(joins)
+    def _():
+        keep(o_src.at[head], o_buf.at[me], OUT)
 
     await_bytes(proj_buf.at[pl.ds(QG, 2)], recv_sem.at[PROJ_KV])
     new_k, new_v = proj_buf[QG].astype(F32), proj_buf[QG + 1].astype(F32)
     for s in range(STEPS):
-        nk_ref[s] = new_k[s * ROWS : (s + 1) * ROWS].astype(BF16)
-        nv_ref[s] = new_v[s * ROWS : (s + 1) * ROWS].astype(BF16)
-
-    @pl.when(owns)
+        out_ref[s, :, width : width + HD] = new_k[s * ROWS : (s + 1) * ROWS].astype(BF16)
+        out_ref[s, :, width + HD :] = new_v[s * ROWS : (s + 1) * ROWS].astype(BF16)
+
+    @pl.when(joins)
     def _():
         second = lax.broadcasted_iota(jnp.int32, (M, 1), 0) >= ROWS
-        q = proj_src[...].astype(F32)
+        q = proj_buf[head].astype(F32)
         k0 = jnp.concatenate([new_k[:ROWS]] * 2, axis=0)
         k1 = jnp.concatenate([new_k[ROWS:]] * 2, axis=0)
         v0 = jnp.concatenate([new_v[:ROWS]] * 2, axis=0)
@@ -285,8 +311,8 @@
             joined += share[:, c : c + 1] * o_buf[c].astype(F32)
         ho_src[...] = (joined * over).astype(BF16)
         for to, _, _ in others():
-            send(ho_src, ho_buf.at[mine], HO, HO, ctx=to)
-        keep(ho_src, ho_buf.at[mine], HO)
+            send(ho_src, ho_buf.at[head], HO, HO, ctx=to)
+        keep(ho_src, ho_buf.at[head], HO)
 
     load_wo.wait()
     await_bytes(ho_buf, recv_sem.at[HO])
@@ -298,34 +324,46 @@
     await_bytes(fin_buf.at[pl.ds(0, ntp - 1)], recv_sem.at[FIN])
     att = jnp.sum(fin_buf[...].astype(F32), axis=0)
     for s in range(STEPS):
-        att_ref[s] = att[s * ROWS : (s + 1) * ROWS].astype(BF16)
-
-    @pl.when(owns)
+        out_ref[s, :, :width] = att[s * ROWS : (s + 1) * ROWS].astype(BF16)
+
+    @pl.when(own_sum)
     def _():
         await_bytes(part_src.at[pl.ds(0, QG - 1)], send_sem.at[PART])
         await_bytes(sq_buf.at[pl.ds(0, QG - 1)], send_sem.at[SQ])
-        await_bytes(o_buf.at[pl.ds(0, nctx - 1)], send_sem.at[PROJ])
+
+    @pl.when(jnp.logical_not(own_sum))
+    def _():
+        await_bytes(part_src.at[pl.ds(0, QG)], send_sem.at[PART])
+        await_bytes(sq_buf.at[pl.ds(0, QG)], send_sem.at[SQ])
+
+    @pl.when(own_kv)
+    def _():
+        await_bytes(part_src.at[pl.ds(0, 1)], send_sem.at[PART_KV])
+
+    @pl.when(jnp.logical_not(own_kv))
+    def _():
+        await_bytes(part_src.at[pl.ds(0, 2)], send_sem.at[PART_KV])
+
+    for does, phase in ((sums, PROJ), (sums_kv, PROJ_KV)):
+
+        @pl.when(jnp.logical_and(does, parity == 1))
+        def _():
+            await_bytes(o_buf.at[pl.ds(0, nctx - 1)], send_sem.at[phase])
+
+        @pl.when(jnp.logical_and(does, parity == 0))
+        def _():
+            await_bytes(o_buf, send_sem.at[phase])
+
+    @pl.when(joins)
+    def _():
         await_bytes(st_src.at[pl.ds(0, QG - 1)], send_sem.at[ST])
         await_bytes(o_src.at[pl.ds(0, QG - 1)], send_sem.at[OUT])
         await_bytes(o_buf.at[pl.ds(0, nctx - 1)], send_sem.at[HO])
 
-    @pl.when(jnp.logical_not(owns))
-    def _():
-        await_bytes(part_src.at[pl.ds(0, QG)], send_sem.at[PART])
-        await_bytes(sq_buf.at[pl.ds(0, QG)], send_sem.at[SQ])
+    @pl.when(jnp.logical_not(joins))
+    def _():
         await_bytes(st_src, send_sem.at[ST])
         await_bytes(o_src, send_sem.at[OUT])
-
-    owns_kv = jnp.logical_or(me == KEY_OWNER, me == VALUE_OWNER)
-
-    @pl.when(owns_kv)
-    def _():
-        await_bytes(part_src.at[pl.ds(0, 1)], send_sem.at[PART_KV])
-        await_bytes(o_buf.at[pl.ds(0, nctx - 1)], send_sem.at[PROJ_KV])
-
-    @pl.when(jnp.logical_not(owns_kv))
-    def _():
-        await_bytes(part_src.at[pl.ds(0, 2)], send_sem.at[PART_KV])
 
     await_bytes(fin_buf.at[pl.ds(0, ntp - 1)], send_sem.at[FIN])
 
@@ -336,16 +374,11 @@
     cached = key_cache.shape[1]
     hbm = pl.BlockSpec(memory_space=pltpu.HBM)
     vmem = pl.BlockSpec(memory_space=pltpu.VMEM)
-    shapes = (
-        jax.ShapeDtypeStruct((STEPS, ROWS, width), BF16),
-        jax.ShapeDtypeStruct((STEPS, ROWS, HD), BF16),
-        jax.ShapeDtypeStruct((STEPS, ROWS, HD), BF16),
-    )
     results = pl.pallas_call(
         functools.partial(kernel, nctx, ntp),
-        out_shape=shapes,
+        out_shape=jax.ShapeDtypeStruct((STEPS, ROWS, width + 2 * HD), BF16),
         in_specs=[hbm] * 8,
-        out_specs=(vmem,) * 3,
+        out_specs=vmem,
         scratch_shapes=[
             pltpu.VMEM((STEPS, ROWS, depth), BF16),
             pltpu.VMEM((1, depth), F32),
@@ -394,7 +427,11 @@
             )
         )
     )
-    return results
+    return (
+        results[:, :, :width],
+        results[:, :, width : width + HD],
+        results[:, :, width + HD :],
+    )
 
 
 def solution(mesh):

time: 46.3 us -> 42.6 us (0.920)
  Pallas kernels: 43.7 us -> 40.6 us
  local copies, waits for them, and re-layouts: 1.79 us -> 1.21 us
    pallas_call x1, Pallas kernels: 43.7 us -> 40.6 us  [local(): pl.pallas_call(functools.partial(kernel, nctx, ntp), out_shape=jax.ShapeD...]
    unnamed x3 -> x0, local copies, waits for them, and re-layouts: 1.79 us -> none
    slice x0 -> x2, local copies, waits for them, and re-layouts: none -> 1.21 us  [the longest x1 0.61 us: local(): results[:, :, :width]]
where the time goes in v3:
time: 42.6 us; the launch traced here: 42.4 us
  Pallas kernels  40.6 us (95%)
  local copies, waits for them, and re-layouts  1.21 us (3%)
  between operations  0.64 us (2%)
    pallas_call x1, Pallas kernels, local(): pl.pallas_call(functools.partial(kernel, nctx, ntp), out_shape=jax.ShapeD...  40.6 us

profile of v3, /device:TPU:1, one launch (start us, length us, event | category | flops | bytes accessed | tf_op | source)
XLA Modules:
  0.0 42.4 jit_solution(3162659036464201896)
XLA Ops:
  0.6 40.6 %shard_map.103 = bf16[2,8,768]{2,1,0:T(8,128)(2,1)S(1)} custom-call(bf16[2,8,512]{2,1,0:T(8,128)(2,1)} %x_hbm.1, f32[1,512]{1,0:T(1,128)} %bitcast.1, bf16[512,2048]{1,0:T(8,128)(2,1)} %wq_hbm.1, bf16[512,128]{1,0:T(8,128)(2,1)} %wk_hbm.1, bf16[512,128]{1,0:T(8,128)(2,1)} %wv_hbm.1, bf16[2048,512]{1,0:T(8,128)(2,1)} %wo_hbm.1, bf16[8,1024,128]{2,1,0:T(8,128)(2,1)} %kc_hbm.1, ...), custom_call_target="tpu_custom_call" | custom-call | tf_op jit(solution)/shard_map/pallas_call | solution.py:377
  41.2 0.6 %fusion = (bf16[2,8,128]{2,1,0:T(8,128)(2,1)}, bf16[2,8,128]{2,1,0:T(8,128)(2,1)}) fusion(bf16[2,8,768]{2,1,0:T(8,128)(2,1)S(1)} %shard_map.103), kind=kLoop, calls=%fused_computation | loop fusion | bytes 16384 | tf_op jit(solution)/shard_map/slice | solution.py:433
  41.8 0.6 %slice.9 = bf16[2,8,512]{2,1,0:T(8,128)(2,1)} slice(bf16[2,8,768]{2,1,0:T(8,128)(2,1)S(1)} %shard_map.103), slice={[0:2], [0:8], [0:512]} | slice | bytes 32768 | tf_op jit(solution)/shard_map/slice | solution.py:431

commit v4 on v3

--- a/solution.py
+++ b/solution.py
@@ -22,6 +22,12 @@
     ((dy, dz) for dy in range(4) for dz in range(8) if (dy, dz) != (0, 0)),
     key=lambda step: -(min(step[0], 4 - step[0]) + min(step[1], 8 - step[1])),
 )
+def head_of(y, z):
+    near = lax.rem(z + 2, 8)
+    low = jnp.where(near < 6, y * 6 + near, QG)
+    return jnp.where(y < 2, low, jnp.where(y == 3, jnp.where(z < 3, 12 + z, QG), 15 + z))
+
+
 def kernel(
     nctx,
     ntp,
@@ -40,6 +46,7 @@
     wkv_v,
     wo_v,
     kc_v,
+    kt_v,
     vc_v,
     sq_src,
     sq_buf,
@@ -78,18 +85,16 @@
     own_sum = jnp.logical_and(sums, parity == 1)
     sibling_sum = jnp.logical_and(core == 0, parity == 0)
     group_tp = chip_tp + parity
-    near = lax.rem(z + 1, 8)
-    head = y * 4 + near
-    joins = near < 4
+    head = head_of(y, z)
+    joins = head < QG
 
     def others():
         for dy, dz in STEPS_AWAY:
             ty, tz = lax.rem(y + dy, 4), lax.rem(z + dz, 8)
             yield ty * 8 + tz, ty, tz
 
-    tp_others = [
-        lax.rem(tp + i, ntp) for i in sorted(range(1, ntp), key=lambda i: abs(i - ntp / 2))
-    ]
+    x = tp // 2
+    tp_steps = [(i, k) for k in (1, 0) for i in (2, 1, 3, 0)]
 
     barrier = pltpu.get_barrier_semaphore()
 
@@ -102,8 +107,8 @@
         def _():
             pl.semaphore_signal(barrier, inc=1, device_id={"ctx": me, "tp": group_tp})
 
-    for to in tp_others:
-        pl.semaphore_signal(barrier, inc=1, device_id={"tp": to})
+    for i in range(1, ntp):
+        pl.semaphore_signal(barrier, inc=1, device_id={"tp": lax.rem(tp + i, ntp)})
 
     def load(i, src, dst):
         copy = pltpu.make_async_copy(src, dst, load_sem.at[i])
@@ -137,12 +142,12 @@
 
     load_x.wait()
     load_gain.wait()
-    x = jnp.concatenate([x_v[0].astype(F32), x_v[1].astype(F32)], axis=0)
-    normed = (x * gain_v[...]).astype(BF16)
+    hidden = jnp.concatenate([x_v[0].astype(F32), x_v[1].astype(F32)], axis=0)
+    normed = (hidden * gain_v[...]).astype(BF16)
     diagonal = lax.broadcasted_iota(jnp.int32, (M, HD), 0) == lax.broadcasted_iota(
         jnp.int32, (M, HD), 1
     )
-    squares = jnp.sum(x * x, axis=1, keepdims=True)
+    squares = jnp.sum(hidden * hidden, axis=1, keepdims=True)
     sq_src[...] = jnp.sum(jnp.where(diagonal, squares, 0.0), axis=0, keepdims=True)
     for copy in load_q:
         copy.wait()
@@ -166,13 +171,16 @@
     def _():
         pl.semaphore_wait(barrier, QG + ntp - 1)
 
-    for to, ty, tz in others():
-
-        @pl.when(lax.rem(ty + tz, 2) == core)
-        def _():
-            h = ty * 4 + tz // 2
-            send(part_src.at[h], part_buf.at[me], PART, PART, ctx=to, tp=chip_tp + 1)
-            send(sq_src, sq_buf.at[me], SQ, SQ, ctx=to, tp=chip_tp + 1)
+    for odd in range(2):
+
+        @pl.when(lax.rem(core + parity, 2) == odd)
+        def _():
+            for dy, dz in STEPS_AWAY:
+                if (dy + dz) % 2 == odd:
+                    ty, tz = lax.rem(y + dy, 4), lax.rem(z + dz, 8)
+                    to, h = ty * 8 + tz, ty * 4 + tz // 2
+                    send(part_src.at[h], part_buf.at[me], PART, PART, ctx=to, tp=chip_tp + 1)
+                    send(sq_src, sq_buf.at[me], SQ, SQ, ctx=to, tp=chip_tp + 1)
 
     @pl.when(sibling_sum)
     def _():
@@ -183,6 +191,37 @@
     def _():
         keep(part_src.at[tile], part_buf.at[me], PART)
         keep(sq_src, sq_buf.at[me], SQ)
+
+    load_kc.wait()
+
+    @pl.loop(0, ROWS)
+    def _(r):
+        kt_v[r] = jnp.transpose(kc_v[r])
+
+    def scale_of_rows():
+        total = jnp.sum(sq_buf[...], axis=0)
+        total = jnp.sum(jnp.where(diagonal, total, 0.0), axis=1, keepdims=True)
+        return lax.rsqrt(total / (depth * nctx) + 1e-05)
+
+    def broadcast(src, dst, phase):
+        for to, _, _ in others():
+            send(src, dst, phase, phase, ctx=to, tp=group_tp)
+
+        @pl.when(parity == 0)
+        def _():
+            send(src, dst, phase, phase, tp=group_tp)
+
+        @pl.when(parity == 1)
+        def _():
+            keep(src, dst, phase)
+
+    @pl.when(sums)
+    def _():
+        await_bytes(sq_buf, recv_sem.at[SQ])
+        scaling = scale_of_rows()
+        await_bytes(part_buf, recv_sem.at[PART])
+        proj_src[...] = (scaling * jnp.sum(part_buf[...], axis=0)).astype(BF16)
+        broadcast(proj_src, proj_buf.at[tile], PROJ)
 
     own_kv = jnp.logical_and(sums_kv, own_sum)
     for i in range(2):
@@ -197,38 +236,9 @@
         def _():
             send(part_src.at[QG + i], kv_buf.at[me], PART_KV, PART_KV, ctx=to, tp=chip_tp + 1)
 
-    def broadcast(src, dst, phase):
-        for to, _, _ in others():
-            send(src, dst, phase, phase, ctx=to, tp=group_tp)
-
-        @pl.when(parity == 0)
-        def _():
-            send(src, dst, phase, phase, tp=group_tp)
-
-        @pl.when(parity == 1)
-        def _():
-            keep(src, dst, phase)
-
-    @pl.when(sums)
-    def _():
-        await_bytes(sq_buf, recv_sem.at[SQ])
-        total = jnp.sum(sq_buf[...], axis=0)
-        total = jnp.sum(jnp.where(diagonal, total, 0.0), axis=1, keepdims=True)
-        scaling = lax.rsqrt(total / (depth * nctx) + 1e-05)
-        await_bytes(part_buf, recv_sem.at[PART])
-        proj_src[...] = (scaling * jnp.sum(part_buf[...], axis=0)).astype(BF16)
-        broadcast(proj_src, proj_buf.at[tile], PROJ)
-
-        @pl.when(sums_kv)
-        def _():
-            await_bytes(kv_buf, recv_sem.at[PART_KV])
-            kv_src[...] = (scaling * jnp.sum(kv_buf[...], axis=0)).astype(BF16)
-            broadcast(kv_src, proj_buf.at[QG + y], PROJ_KV)
-
     await_bytes(proj_buf.at[pl.ds(0, QG)], recv_sem.at[PROJ])
     for h in range(QG):
         q_rows[pl.ds(h * M, M), :] = proj_buf[h].astype(F32)
-    load_kc.wait()
     score_scale = LOG2E / float(HD) ** 0.5
     lane = lax.broadcasted_iota(jnp.int32, (QG, HD), 1)
     stats = jnp.zeros((QG, HD), F32)
@@ -237,9 +247,7 @@
         q = jnp.concatenate(
             [q_rows[pl.ds(s * ROWS + r, QG, stride=M), :] for s in range(STEPS)], axis=0
         ).astype(BF16)
-        score = lax.dot_general(
-            q, kc_v[r], (((1,), (1,)), ((), ())), preferred_element_type=F32
-        )
+        score = jnp.dot(q, kt_v[r], preferred_element_type=F32)
         top = jnp.max(score, axis=1, keepdims=True)
         weight = jnp.exp2((score - top) * score_scale)
         total = jnp.sum(weight, axis=1, keepdims=True)
@@ -252,11 +260,11 @@
         st_src[h] = stats[h : h + 1]
 
     for to, ty, tz in others():
-        to_near = lax.rem(tz + 1, 8)
-
-        @pl.when(to_near < 4)
-        def _():
-            send(st_src.at[ty * 4 + to_near], st_buf.at[me], ST, ST, ctx=to)
+        h = head_of(ty, tz)
+
+        @pl.when(h < QG)
+        def _():
+            send(st_src.at[h], st_buf.at[me], ST, ST, ctx=to)
 
     @pl.when(joins)
     def _():
@@ -271,15 +279,21 @@
         o_src[h] = o_rows[pl.ds(h * M, M), :].astype(BF16)
 
     for to, ty, tz in others():
-        to_near = lax.rem(tz + 1, 8)
-
-        @pl.when(to_near < 4)
-        def _():
-            send(o_src.at[ty * 4 + to_near], o_buf.at[me], OUT, OUT, ctx=to)
+        h = head_of(ty, tz)
+
+        @pl.when(h < QG)
+        def _():
+            send(o_src.at[h], o_buf.at[me], OUT, OUT, ctx=to)
 
     @pl.when(joins)
     def _():
         keep(o_src.at[head], o_buf.at[me], OUT)
+
+    @pl.when(sums_kv)
+    def _():
+        await_bytes(kv_buf, recv_sem.at[PART_KV])
+        kv_src[...] = (scale_of_rows() * jnp.sum(kv_buf[...], axis=0)).astype(BF16)
+        broadcast(kv_src, proj_buf.at[QG + y], PROJ_KV)
 
     await_bytes(proj_buf.at[pl.ds(QG, 2)], recv_sem.at[PROJ_KV])
     new_k, new_v = proj_buf[QG].astype(F32), proj_buf[QG + 1].astype(F32)
@@ -310,8 +324,16 @@
         for c in range(nctx):
             joined += share[:, c : c + 1] * o_buf[c].astype(F32)
         ho_src[...] = (joined * over).astype(BF16)
+        @pl.when(me != 0)
+        def _():
+            send(ho_src, ho_buf.at[head], HO, HO, ctx=0)
+
         for to, _, _ in others():
-            send(ho_src, ho_buf.at[head], HO, HO, ctx=to)
+
+            @pl.when(to != 0)
+            def _():
+                send(ho_src, ho_buf.at[head], HO, HO, ctx=to)
+
         keep(ho_src, ho_buf.at[head], HO)
 
     load_wo.wait()
@@ -319,8 +341,16 @@
     heads_out = jnp.concatenate([ho_buf[h] for h in range(QG)], axis=1)
     y = jnp.dot(heads_out, wo_v[...], preferred_element_type=F32)
     fin_buf[tp] = y.astype(BF16)
-    for to in tp_others:
-        send(fin_buf.at[tp], fin_buf.at[tp], FIN, FIN, tp=to)
+    for i, k in tp_steps:
+        to = 2 * lax.rem(x + i, 4) + k
+        if i == 0:
+
+            @pl.when(to != tp)
+            def _():
+                send(fin_buf.at[tp], fin_buf.at[tp], FIN, FIN, tp=to)
+
+        else:
+            send(fin_buf.at[tp], fin_buf.at[tp], FIN, FIN, tp=to)
     await_bytes(fin_buf.at[pl.ds(0, ntp - 1)], recv_sem.at[FIN])
     att = jnp.sum(fin_buf[...].astype(F32), axis=0)
     for s in range(STEPS):
@@ -386,6 +416,7 @@
             pltpu.VMEM((depth, 2 * HD), BF16),
             pltpu.VMEM((QG * HD, width), BF16),
             pltpu.VMEM((ROWS, cached, HD), BF16),
+            pltpu.VMEM((ROWS, HD, cached), BF16),
             pltpu.VMEM((ROWS, cached, HD), BF16),
             pltpu.VMEM((1, HD), F32),
             pltpu.VMEM((nctx, 1, HD), F32),

time: 42.6 us -> 40.7 us (0.955)
  Pallas kernels: 40.6 us -> 38.7 us
    pallas_call x1, Pallas kernels: 40.6 us -> 38.7 us  [local(): pl.pallas_call(functools.partial(kernel, nctx, ntp), out_shape=jax.ShapeD...]
where the time goes in v4:
time: 40.7 us; the launch traced here: 40.5 us
  Pallas kernels  38.7 us (95%)
  local copies, waits for them, and re-layouts  1.21 us (3%)
  between operations  0.64 us (2%)
    pallas_call x1, Pallas kernels, local(): pl.pallas_call(functools.partial(kernel, nctx, ntp), out_shape=jax.ShapeD...  38.7 us

profile of v4, /device:TPU:1, one launch (start us, length us, event | category | flops | bytes accessed | tf_op | source)
XLA Modules:
  0.0 40.5 jit_solution(13331496198249612333)
XLA Ops:
  0.6 38.7 %shard_map.103 = bf16[2,8,768]{2,1,0:T(8,128)(2,1)S(1)} custom-call(bf16[2,8,512]{2,1,0:T(8,128)(2,1)} %x_hbm.1, f32[1,512]{1,0:T(1,128)} %bitcast.1, bf16[512,2048]{1,0:T(8,128)(2,1)} %wq_hbm.1, bf16[512,128]{1,0:T(8,128)(2,1)} %wk_hbm.1, bf16[512,128]{1,0:T(8,128)(2,1)} %wv_hbm.1, bf16[2048,512]{1,0:T(8,128)(2,1)} %wo_hbm.1, bf16[8,1024,128]{2,1,0:T(8,128)(2,1)} %kc_hbm.1, ...), custom_call_target="tpu_custom_call" | custom-call | tf_op jit(solution)/shard_map/pallas_call | solution.py:407
  39.3 0.6 %fusion = (bf16[2,8,128]{2,1,0:T(8,128)(2,1)}, bf16[2,8,128]{2,1,0:T(8,128)(2,1)}) fusion(bf16[2,8,768]{2,1,0:T(8,128)(2,1)S(1)} %shard_map.103), kind=kLoop, calls=%fused_computation | loop fusion | bytes 16384 | tf_op jit(solution)/shard_map/slice | solution.py:464
  39.9 0.6 %slice.9 = bf16[2,8,512]{2,1,0:T(8,128)(2,1)} slice(bf16[2,8,768]{2,1,0:T(8,128)(2,1)S(1)} %shard_map.103), slice={[0:2], [0:8], [0:512]} | slice | bytes 32768 | tf_op jit(solution)/shard_map/slice | solution.py:462

commit v5 on v4

--- a/solution.py
+++ b/solution.py
@@ -259,17 +259,6 @@
     for h in range(QG):
         st_src[h] = stats[h : h + 1]
 
-    for to, ty, tz in others():
-        h = head_of(ty, tz)
-
-        @pl.when(h < QG)
-        def _():
-            send(st_src.at[h], st_buf.at[me], ST, ST, ctx=to)
-
-    @pl.when(joins)
-    def _():
-        keep(st_src.at[head], st_buf.at[me], ST)
-
     load_vc.wait()
     for r in range(ROWS):
         out = jnp.dot(p_v[r], vc_v[r], preferred_element_type=F32) * inverse[r]
@@ -283,10 +272,12 @@
 
         @pl.when(h < QG)
         def _():
+            send(st_src.at[h], st_buf.at[me], ST, ST, ctx=to)
             send(o_src.at[h], o_buf.at[me], OUT, OUT, ctx=to)
 
     @pl.when(joins)
     def _():
+        keep(st_src.at[head], st_buf.at[me], ST)
         keep(o_src.at[head], o_buf.at[me], OUT)
 
     @pl.when(sums_kv)

time: 40.7 us -> 40.6 us (level)
  no operation moved by 1% of the time
where the time goes in v5:
time: 40.6 us; the launch traced here: 40.4 us
  Pallas kernels  38.5 us (95%)
  local copies, waits for them, and re-layouts  1.21 us (3%)
  between operations  0.64 us (2%)
    pallas_call x1, Pallas kernels, local(): pl.pallas_call(functools.partial(kernel, nctx, ntp), out_shape=jax.ShapeD...  38.5 us

profile of v5, /device:TPU:1, one launch (start us, length us, event | category | flops | bytes accessed | tf_op | source)
XLA Modules:
  0.0 40.4 jit_solution(16059606821686998559)
XLA Ops:
  0.6 38.5 %shard_map.103 = bf16[2,8,768]{2,1,0:T(8,128)(2,1)S(1)} custom-call(bf16[2,8,512]{2,1,0:T(8,128)(2,1)} %x_hbm.1, f32[1,512]{1,0:T(1,128)} %bitcast.1, bf16[512,2048]{1,0:T(8,128)(2,1)} %wq_hbm.1, bf16[512,128]{1,0:T(8,128)(2,1)} %wk_hbm.1, bf16[512,128]{1,0:T(8,128)(2,1)} %wv_hbm.1, bf16[2048,512]{1,0:T(8,128)(2,1)} %wo_hbm.1, bf16[8,1024,128]{2,1,0:T(8,128)(2,1)} %kc_hbm.1, ...), custom_call_target="tpu_custom_call" | custom-call | tf_op jit(solution)/shard_map/pallas_call | solution.py:398
  39.2 0.6 %fusion = (bf16[2,8,128]{2,1,0:T(8,128)(2,1)}, bf16[2,8,128]{2,1,0:T(8,128)(2,1)}) fusion(bf16[2,8,768]{2,1,0:T(8,128)(2,1)S(1)} %shard_map.103), kind=kLoop, calls=%fused_computation | loop fusion | bytes 16384 | tf_op jit(solution)/shard_map/slice | solution.py:455
  39.8 0.6 %slice.9 = bf16[2,8,512]{2,1,0:T(8,128)(2,1)} slice(bf16[2,8,768]{2,1,0:T(8,128)(2,1)S(1)} %shard_map.103), slice={[0:2], [0:8], [0:512]} | slice | bytes 32768 | tf_op jit(solution)/shard_map/slice | solution.py:453

commit v6 on v5

--- a/solution.py
+++ b/solution.py
@@ -149,20 +149,20 @@
     )
     squares = jnp.sum(hidden * hidden, axis=1, keepdims=True)
     sq_src[...] = jnp.sum(jnp.where(diagonal, squares, 0.0), axis=0, keepdims=True)
-    for copy in load_q:
+    half = depth // 2
+    for copy in load_q[:2]:
+        copy.wait()
+    part = jnp.dot(normed[:, :half], wq_v[:half, :], preferred_element_type=F32)
+    for copy in load_q[2:]:
         copy.wait()
     load_k.wait()
     load_v.wait()
     load_kc = load(0, kc_hbm, kc_v)
     load_vc = load(1, vc_hbm, vc_v)
     load_wo = load(2, wo_hbm, wo_v)
-    part = jnp.dot(normed, wq_v[...], preferred_element_type=F32)
+    part += jnp.dot(normed[:, half:], wq_v[half:, :], preferred_element_type=F32)
     for h in range(QG):
         part_src[h] = part[:, h * HD : (h + 1) * HD]
-    part = jnp.dot(normed, wkv_v[...], preferred_element_type=F32)
-    for h in range(2):
-        part_src[QG + h] = part[:, h * HD : (h + 1) * HD]
-
     @pl.when(own_sum)
     def _():
         pl.semaphore_wait(barrier, QG - 1 + ntp - 1)
@@ -191,6 +191,10 @@
     def _():
         keep(part_src.at[tile], part_buf.at[me], PART)
         keep(sq_src, sq_buf.at[me], SQ)
+
+    part = jnp.dot(normed, wkv_v[...], preferred_element_type=F32)
+    for h in range(2):
+        part_src[QG + h] = part[:, h * HD : (h + 1) * HD]
 
     load_kc.wait()
 

time: 40.6 us -> 40.6 us (level)
  no operation moved by 1% of the time
where the time goes in v6:
time: 40.6 us; the launch traced here: 40.4 us
  Pallas kernels  38.5 us (95%)
  local copies, waits for them, and re-layouts  1.21 us (3%)
  between operations  0.64 us (2%)
    pallas_call x1, Pallas kernels, local(): pl.pallas_call(functools.partial(kernel, nctx, ntp), out_shape=jax.ShapeD...  38.5 us

profile of v6, /device:TPU:1, one launch (start us, length us, event | category | flops | bytes accessed | tf_op | source)
XLA Modules:
  0.0 40.4 jit_solution(16380484429596667586)
XLA Ops:
  0.6 38.5 %shard_map.103 = bf16[2,8,768]{2,1,0:T(8,128)(2,1)S(1)} custom-call(bf16[2,8,512]{2,1,0:T(8,128)(2,1)} %x_hbm.1, f32[1,512]{1,0:T(1,128)} %bitcast.1, bf16[512,2048]{1,0:T(8,128)(2,1)} %wq_hbm.1, bf16[512,128]{1,0:T(8,128)(2,1)} %wk_hbm.1, bf16[512,128]{1,0:T(8,128)(2,1)} %wv_hbm.1, bf16[2048,512]{1,0:T(8,128)(2,1)} %wo_hbm.1, bf16[8,1024,128]{2,1,0:T(8,128)(2,1)} %kc_hbm.1, ...), custom_call_target="tpu_custom_call" | custom-call | tf_op jit(solution)/shard_map/pallas_call | solution.py:402
  39.2 0.6 %fusion = (bf16[2,8,128]{2,1,0:T(8,128)(2,1)}, bf16[2,8,128]{2,1,0:T(8,128)(2,1)}) fusion(bf16[2,8,768]{2,1,0:T(8,128)(2,1)S(1)} %shard_map.103), kind=kLoop, calls=%fused_computation | loop fusion | bytes 16384 | tf_op jit(solution)/shard_map/slice | solution.py:459
  39.8 0.6 %slice.9 = bf16[2,8,512]{2,1,0:T(8,128)(2,1)} slice(bf16[2,8,768]{2,1,0:T(8,128)(2,1)S(1)} %shard_map.103), slice={[0:2], [0:8], [0:512]} | slice | bytes 32768 | tf_op jit(solution)/shard_map/slice | solution.py:457

commit v7 on v6

--- a/solution.py
+++ b/solution.py
@@ -180,6 +180,9 @@
                     ty, tz = lax.rem(y + dy, 4), lax.rem(z + dz, 8)
                     to, h = ty * 8 + tz, ty * 4 + tz // 2
                     send(part_src.at[h], part_buf.at[me], PART, PART, ctx=to, tp=chip_tp + 1)
+            for dy, dz in STEPS_AWAY:
+                if (dy + dz) % 2 == odd:
+                    to = lax.rem(y + dy, 4) * 8 + lax.rem(z + dz, 8)
                     send(sq_src, sq_buf.at[me], SQ, SQ, ctx=to, tp=chip_tp + 1)
 
     @pl.when(sibling_sum)

time: 40.6 us -> 42.3 us (1.042)
  Pallas kernels: 38.5 us -> 40.3 us
    pallas_call x1, Pallas kernels: 38.5 us -> 40.3 us  [local(): pl.pallas_call(functools.partial(kernel, nctx, ntp), out_shape=jax.ShapeD...]
where the time goes in v7:
time: 42.3 us; the launch traced here: 42.1 us
  Pallas kernels  40.3 us (95%)
  local copies, waits for them, and re-layouts  1.21 us (3%)
  between operations  0.64 us (2%)
    pallas_call x1, Pallas kernels, local(): pl.pallas_call(functools.partial(kernel, nctx, ntp), out_shape=jax.ShapeD...  40.3 us

profile of v7, /device:TPU:1, one launch (start us, length us, event | category | flops | bytes accessed | tf_op | source)
XLA Modules:
  0.0 42.1 jit_solution(6737034390265335426)
XLA Ops:
  0.6 40.3 %shard_map.103 = bf16[2,8,768]{2,1,0:T(8,128)(2,1)S(1)} custom-call(bf16[2,8,512]{2,1,0:T(8,128)(2,1)} %x_hbm.1, f32[1,512]{1,0:T(1,128)} %bitcast.1, bf16[512,2048]{1,0:T(8,128)(2,1)} %wq_hbm.1, bf16[512,128]{1,0:T(8,128)(2,1)} %wk_hbm.1, bf16[512,128]{1,0:T(8,128)(2,1)} %wv_hbm.1, bf16[2048,512]{1,0:T(8,128)(2,1)} %wo_hbm.1, bf16[8,1024,128]{2,1,0:T(8,128)(2,1)} %kc_hbm.1, ...), custom_call_target="tpu_custom_call" | custom-call | tf_op jit(solution)/shard_map/pallas_call | solution.py:405
  40.9 0.6 %fusion = (bf16[2,8,128]{2,1,0:T(8,128)(2,1)}, bf16[2,8,128]{2,1,0:T(8,128)(2,1)}) fusion(bf16[2,8,768]{2,1,0:T(8,128)(2,1)S(1)} %shard_map.103), kind=kLoop, calls=%fused_computation | loop fusion | bytes 16384 | tf_op jit(solution)/shard_map/slice | solution.py:462
  41.5 0.6 %slice.9 = bf16[2,8,512]{2,1,0:T(8,128)(2,1)} slice(bf16[2,8,768]{2,1,0:T(8,128)(2,1)S(1)} %shard_map.103), slice={[0:2], [0:8], [0:512]} | slice | bytes 32768 | tf_op jit(solution)/shard_map/slice | solution.py:460
